TPU v7x, 128 devices: a whole 4x4x4 slice. The times are simulated.
128 devices in a mesh: radial: 32 (over z, x, core), chan: 4 (over y).
Axes of the slice: x: 4, y: 4, z: 4, core: 2. Of those that a mesh axis runs over, the one named last changes fastest.
Arguments:
- outer_wave: float32 [2, 1200, 8192], P(None, 'chan', 'radial'), may hold values from -6 to 6
- inner_wave: float32 [2, 30720], P(None, 'radial'), may hold values from -1.5 to 1.5
- inner_ham: bfloat16 [30720, 30720], P('radial', 'chan'), may hold values from -15 to 15
- surface: bfloat16 [2, 1200, 30720], P(None, 'chan', 'radial'), may hold values from -0.046875 to 0.046875
- dipole: bfloat16 [1200, 1200], P('chan'), as said below
- ang_mom: int32 [1200], replicated, may hold values from 0 to 23
- target: int32 [1200], replicated, may hold values from 0 to 7
- couple_mask: int32 [8, 8], replicated, may hold values from 0 to 1, as said below
Outputs:
- outer_next: float32 [2, 1200, 8192], P(None, 'chan', 'radial')
- inner_next: float32 [2, 30720], P(None, 'radial')
Inputs may be any that keep to these rules, and one draw needn't show every extreme that they name: dipole is symmetric. couple_mask is symmetric with ones on its diagonal.
All inputs are finite; a program needn't handle non-finite values.
Results may differ from a plain program's by a relative error of at most 0.0054.
Values may be sent and summed in bfloat16 or wider, within the bound.
A program may use at most 128 MiB of HBM per device.

v0:
```python
import jax
import jax.numpy as jnp
from jax import lax
from jax.sharding import PartitionSpec as P

ORDER = 8


time_step = 0.008
grid_step = 0.08
inner_radius = 20.0
surface_gain = 16.0 / (24.0 * grid_step * grid_step)


def from_root(array, axis, root):
    mine = lax.axis_index(axis) == root
    return lax.psum(jnp.where(mine, array, jnp.zeros_like(array)), axis)


def with_halo(cells, sides, width):
    for axis, dim in sides:
        count = lax.axis_size(axis)
        ends = count - 1
        head = lax.slice_in_dim(cells, 0, width, axis=dim)
        tail = lax.slice_in_dim(cells, cells.shape[dim] - width, cells.shape[dim], axis=dim)
        cells = jnp.concatenate(
            [
                lax.ppermute(tail, axis, [(i, (i + 1) % count) for i in range(ends)]),
                cells,
                lax.ppermute(head, axis, [((i + 1) % count, i) for i in range(ends)]),
            ],
            axis=dim,
        )
    return cells


def local(outer_wave, inner_wave, inner_ham, surface, dipole, ang_mom, target, couple_mask):
    chan_index = lax.axis_index("chan")
    radial_index = lax.axis_index("radial")
    local_chan = dipole.shape[0]
    radial_len = outer_wave.shape[2]
    col_len = inner_ham.shape[1]
    levels = jnp.arange(couple_mask.shape[0])
    hot_all = (target[:, None] == levels[None, :]).astype(jnp.float32)
    hot_mine = lax.dynamic_slice_in_dim(hot_all, chan_index * local_chan, local_chan, 0)
    allowed = jnp.dot(
        jnp.dot(hot_mine, couple_mask.astype(jnp.float32), precision=lax.Precision.HIGHEST),
        hot_all.T,
        precision=lax.Precision.HIGHEST,
    )
    mom_mine = lax.dynamic_slice_in_dim(ang_mom, chan_index * local_chan, local_chan, 0)
    step_l = jnp.abs(mom_mine[:, None] - ang_mom[None, :]) == 1
    coupling = jnp.where(step_l & (allowed > 0.5), dipole, jnp.zeros_like(dipole))
    points = radial_index * radial_len + jnp.arange(radial_len)
    radius = inner_radius + grid_step * (points.astype(jnp.float32) + 1.0)
    lvals = mom_mine.astype(jnp.float32)
    centri = (lvals * (lvals + 1.0) / 2.0)[:, None] / (radius * radius)[None, :]
    outer_term, inner_term = (outer_wave, inner_wave)
    outer_total, inner_total = (outer_wave, inner_wave)
    for order in range(1, ORDER + 1):
        outer_half = outer_term.astype(jnp.bfloat16)
        whole = lax.all_gather(inner_term.astype(jnp.bfloat16), "radial", axis=1, tiled=True)
        own_rows = inner_term.astype(jnp.bfloat16)
        column_block = lax.dynamic_slice_in_dim(whole, chan_index * col_len, col_len, 1)
        ghost_part = jnp.einsum(
            "mci,si->msc", surface, own_rows, preferred_element_type=jnp.float32
        )
        edge = outer_half[:, :, 0:2]
        ghost = lax.psum(ghost_part, "radial")
        edge_vals = from_root(edge, "radial", 0)
        surface_term = surface_gain * jnp.einsum(
            "mci,scm->si", surface, edge_vals, preferred_element_type=jnp.float32
        )
        inner_part = (
            jnp.einsum("ij,sj->si", inner_ham, column_block, preferred_element_type=jnp.float32)
            + surface_term
        )
        inner_apply = lax.psum(inner_part, "chan")
        mixed = jnp.einsum(
            "cb,sbj->scj",
            coupling,
            lax.all_gather(outer_half, "chan", axis=1, tiled=True),
            preferred_element_type=jnp.float32,
        )
        padded = with_halo(outer_term, (("radial", 2),), 2)
        rim = jnp.stack([ghost[1], ghost[0]], axis=-1)
        lower = jnp.where(radial_index == 0, rim, padded[:, :, 0:2])
        padded = jnp.concatenate([lower, padded[:, :, 2:]], axis=-1)
        lap = (
            -padded[..., 0:radial_len]
            + 16.0 * padded[..., 1 : radial_len + 1]
            - 30.0 * padded[..., 2 : radial_len + 2]
            + 16.0 * padded[..., 3 : radial_len + 3]
            - padded[..., 4 : radial_len + 4]
        ) / (12.0 * grid_step * grid_step)
        outer_apply = -0.5 * lap + centri * outer_term + radius * mixed
        factor = time_step / order
        outer_term = jnp.stack([factor * outer_apply[1], -factor * outer_apply[0]])
        inner_term = jnp.stack([factor * inner_apply[1], -factor * inner_apply[0]])
        outer_total = outer_total + outer_term
        inner_total = inner_total + inner_term
    return (outer_total, inner_total)


def solution(mesh):
    placed = (
        P(None, "chan", "radial"),
        P(None, "radial"),
        P("radial", "chan"),
        P(None, "chan", "radial"),
        P("chan", None),
        P(),
        P(),
        P(),
    )
    return jax.shard_map(
        local,
        mesh=mesh,
        in_specs=placed,
        out_specs=(P(None, "chan", "radial"), P(None, "radial")),
        check_vma=False,
    )
```

profile of v0, /device:TPU:1, one launch (start us, length us, event | category | flops | bytes accessed | tf_op | source)
XLA Modules:
  0.0 1712.8 jit_solution(12898118344266520247)
XLA Ops:
  9.6 4.6 collective-permute-start
  17.8 28.1 %all-gather = bf16[32,960,2]{1,2,0:T(2,128)(2,1)S(1)} all-gather(bf16[1,960,2]{1,2,0:T(2,128)(2,1)S(1)} %convert_bitcast_fusion), channel_id=1, replica_groups=mesh['radial'=32,'chan'=4] {'radial'}, dimensions={0}, use_global_device_ids=true | all-gather | bytes 126720 | tf_op jit(solution)/shard_map/all_gather | solution.py:62
  46.3 122.4 %psum.169 = bf16[2,300,2]{2,0,1:T(2,128)(2,1)S(1)} all-reduce(bf16[2,300,2]{2,0,1:T(2,128)(2,1)S(1)} %broadcast_select_fusion.7), channel_id=1, replica_groups=mesh['radial'=32,'chan'=4] {'radial'}, use_global_device_ids=true, to_apply=%region_1.2 | all-reduce | flops 1200 | bytes 4800 | tf_op jit(solution)/shard_map/psum | solution.py:17
  168.8 9.1 fusion.116
  178.4 8.8 psum.170
  187.8 126.4 %all-reduce.3 = (f32[2,2,300]{2,1,0:T(2,128)S(1)}, f32[2,2,300]{2,1,0:T(2,128)S(1)}) all-reduce(f32[2,2,300]{2,1,0:T(2,128)S(1)} %convolution_bitcast_fusion.15, f32[2,2,300]{2,1,0:T(2,128)S(1)} %convolution_bitcast_fusion.14), channel_id=1, replica_groups=mesh['radial'=32,'chan'=4] {'radial'}, use_global_device_ids=true, to_apply=%region_0.1 | all-reduce | flops 2400 | bytes 19200 | tf_op jit(solution)/shard_map/psum | solution.py:69
  330.5 26.2 %all-gather.1 = bf16[32,960,2]{1,2,0:T(2,128)(2,1)S(1)} all-gather(bf16[1,960,2]{1,2,0:T(2,128)(2,1)S(1)} %fusion.146), channel_id=1, replica_groups=mesh['radial'=32,'chan'=4] {'radial'}, dimensions={0}, use_global_device_ids=true | all-gather | bytes 126720 | tf_op jit(solution)/shard_map/all_gather | solution.py:62
  357.3 9.7 fusion.114
  367.9 4.4 collective-permute-start.2
  376.5 4.1 collective-permute-done.3
  392.6 121.8 %all-reduce.6 = (bf16[2,300,2]{2,0,1:T(2,128)(2,1)S(1)}, bf16[2,300,2]{2,0,1:T(2,128)(2,1)S(1)}) all-reduce(bf16[2,300,2]{2,0,1:T(2,128)(2,1)S(1)} %broadcast_select_fusion.6, bf16[2,300,2]{2,0,1:T(2,128)(2,1)S(1)} %broadcast_select_fusion.5), channel_id=1, replica_groups=mesh['radial'=32,'chan'=4] {'radial'}, use_global_device_ids=true, to_apply=%region_4.5 | all-reduce | flops 2400 | bytes 9600 | tf_op jit(solution)/shard_map/psum | solution.py:17
  515.0 6.1 psum.173
  521.1 28.1 %all-gather.2 = bf16[32,960,2]{1,2,0:T(2,128)(2,1)S(1)} all-gather(bf16[1,960,2]{1,2,0:T(2,128)(2,1)S(1)} %fusion.148), channel_id=1, replica_groups=mesh['radial'=32,'chan'=4] {'radial'}, dimensions={0}, use_global_device_ids=true | all-gather | bytes 126720 | tf_op jit(solution)/shard_map/all_gather | solution.py:62
  549.4 9.1 fusion.112
  560.4 4.4 collective-permute-start.4
  565.3 8.2 psum.176
  574.5 118.8 %all-reduce.2 = (f32[2,2,300]{2,1,0:T(2,128)S(1)}, f32[2,2,300]{2,1,0:T(2,128)S(1)}) all-reduce(f32[2,2,300]{2,1,0:T(2,128)S(1)} %convolution_bitcast_fusion.13, f32[2,2,300]{2,1,0:T(2,128)S(1)} %convolution_bitcast_fusion.12), channel_id=1, replica_groups=mesh['radial'=32,'chan'=4] {'radial'}, use_global_device_ids=true, to_apply=%region_6.7 | all-reduce | flops 2400 | bytes 19200 | tf_op jit(solution)/shard_map/psum | solution.py:69
  693.4 26.3 %all-gather.3 = bf16[32,960,2]{1,2,0:T(2,128)(2,1)S(1)} all-gather(bf16[1,960,2]{1,2,0:T(2,128)(2,1)S(1)} %fusion.150), channel_id=1, replica_groups=mesh['radial'=32,'chan'=4] {'radial'}, dimensions={0}, use_global_device_ids=true | all-gather | bytes 126720 | tf_op jit(solution)/shard_map/all_gather | solution.py:62
  724.0 5.5 collective-permute-done.5
  742.3 9.7 fusion.110
  759.1 4.9 collective-permute-done.7
  777.5 123.3 %all-reduce.5 = (bf16[2,300,2]{2,0,1:T(2,128)(2,1)}, bf16[2,300,2]{2,0,1:T(2,128)(2,1)}) all-reduce(bf16[2,300,2]{2,0,1:T(2,128)(2,1)S(1)} %broadcast_select_fusion.4, bf16[2,300,2]{2,0,1:T(2,128)(2,1)} %broadcast_select_fusion.3), channel_id=1, replica_groups=mesh['radial'=32,'chan'=4] {'radial'}, use_global_device_ids=true, to_apply=%region_10.11 | all-reduce | flops 2400 | bytes 9600 | tf_op jit(solution)/shard_map/psum | solution.py:17
  903.0 7.8 psum.179
  911.5 28.4 %all-gather.4 = bf16[32,960,2]{1,2,0:T(2,128)(2,1)S(1)} all-gather(bf16[1,960,2]{1,2,0:T(2,128)(2,1)S(1)} %fusion.152), channel_id=1, replica_groups=mesh['radial'=32,'chan'=4] {'radial'}, dimensions={0}, use_global_device_ids=true | all-gather | bytes 126720 | tf_op jit(solution)/shard_map/all_gather | solution.py:62
  940.7 9.8 fusion.108
  953.0 4.4 collective-permute-start.8
  958.5 6.1 psum.182
  966.4 118.8 %all-reduce.1 = (f32[2,2,300]{2,1,0:T(2,128)S(1)}, f32[2,2,300]{2,1,0:T(2,128)S(1)}) all-reduce(f32[2,2,300]{2,1,0:T(2,128)S(1)} %convolution_bitcast_fusion.11, f32[2,2,300]{2,1,0:T(2,128)S(1)} %convolution_bitcast_fusion.10), channel_id=1, replica_groups=mesh['radial'=32,'chan'=4] {'radial'}, use_global_device_ids=true, to_apply=%region_12.13 | all-reduce | flops 2400 | bytes 19200 | tf_op jit(solution)/shard_map/psum | solution.py:69
  1085.2 26.3 %all-gather.5 = bf16[32,960,2]{1,2,0:T(2,128)(2,1)S(1)} all-gather(bf16[1,960,2]{1,2,0:T(2,128)(2,1)S(1)} %fusion.154), channel_id=1, replica_groups=mesh['radial'=32,'chan'=4] {'radial'}, dimensions={0}, use_global_device_ids=true | all-gather | bytes 126720 | tf_op jit(solution)/shard_map/all_gather | solution.py:62
  1118.2 5.3 collective-permute-done.9
  1123.5 3.7 maximum_maximum_fusion.3
  1137.2 9.8 fusion.106
  1154.1 4.9 collective-permute-done.11
  1172.5 124.3 %all-reduce.4 = (bf16[2,300,2]{2,0,1:T(2,128)(2,1)}, bf16[2,300,2]{2,0,1:T(2,128)(2,1)}) all-reduce(bf16[2,300,2]{2,0,1:T(2,128)(2,1)S(1)} %broadcast_select_fusion.2, bf16[2,300,2]{2,0,1:T(2,128)(2,1)} %broadcast_select_fusion.1), channel_id=1, replica_groups=mesh['radial'=32,'chan'=4] {'radial'}, use_global_device_ids=true, to_apply=%region_16.17 | all-reduce | flops 2400 | bytes 9600 | tf_op jit(solution)/shard_map/psum | solution.py:17
  1299.1 7.8 psum.185
  1307.5 28.4 %all-gather.6 = bf16[32,960,2]{1,2,0:T(2,128)(2,1)S(1)} all-gather(bf16[1,960,2]{1,2,0:T(2,128)(2,1)S(1)} %fusion.156), channel_id=1, replica_groups=mesh['radial'=32,'chan'=4] {'radial'}, dimensions={0}, use_global_device_ids=true | all-gather | bytes 126720 | tf_op jit(solution)/shard_map/all_gather | solution.py:62
  1336.8 9.8 fusion.104
  1349.0 4.4 collective-permute-start.12
  1354.6 6.1 psum.188
  1362.5 119.0 %all-reduce = (f32[2,2,300]{2,1,0:T(2,128)S(1)}, f32[2,2,300]{2,1,0:T(2,128)S(1)}) all-reduce(f32[2,2,300]{2,1,0:T(2,128)S(1)} %convolution_bitcast_fusion.9, f32[2,2,300]{2,1,0:T(2,128)S(1)} %convolution_bitcast_fusion.8), channel_id=1, replica_groups=mesh['radial'=32,'chan'=4] {'radial'}, use_global_device_ids=true, to_apply=%region_18.19 | all-reduce | flops 2400 | bytes 19200 | tf_op jit(solution)/shard_map/psum | solution.py:69
  1481.5 26.3 %all-gather.7 = bf16[32,960,2]{1,2,0:T(2,128)(2,1)S(1)} all-gather(bf16[1,960,2]{1,2,0:T(2,128)(2,1)S(1)} %fusion.158), channel_id=1, replica_groups=mesh['radial'=32,'chan'=4] {'radial'}, dimensions={0}, use_global_device_ids=true | all-gather | bytes 126720 | tf_op jit(solution)/shard_map/all_gather | solution.py:62
  1514.5 5.3 collective-permute-done.13
  1531.7 9.7 fusion.102
  1545.0 120.7 %psum.190 = bf16[2,300,2]{2,0,1:T(2,128)(2,1)S(1)} all-reduce(bf16[2,300,2]{2,0,1:T(2,128)(2,1)} %broadcast_select_fusion), channel_id=1, replica_groups=mesh['radial'=32,'chan'=4] {'radial'}, use_global_device_ids=true, to_apply=%region_22.23 | all-reduce | flops 1200 | bytes 4800 | tf_op jit(solution)/shard_map/psum | solution.py:17
  1672.9 6.0 collective-permute-start.15
  1679.4 8.2 psum.191
  1690.0 4.6 maximum_maximum_fusion.6
  1701.3 4.5 maximum_add_fusion
  (380 shorter events, 176.3 us)
Async XLA Ops:
  7.2 315.6 %all-gather.17.cloned.1.call-start = ((), (), s32[]{:S(2)}) async-start(), calls=%async_computation | async-start | bytes 1536000 | tf_op jit(solution)/shard_map/all_gather | solution.py:82
  9.6 311.0 %collective-permute-start = (f32[2,300,2]{2,0,1:T(2,128)}, f32[2,300,2]{2,0,1:T(2,128)}, u32[]{:S(2)}, u32[]{:S(2)}) collective-permute-start(f32[2,300,2]{2,0,1:T(2,128)} %get-tuple-element.70), channel_id=1, source_target_pairs={{0,4},{4,8},{8,12},{12,16},{16,20},{20,24},{24,28},{28,32},{32,36}... | collective-permute-start | bytes 14408 | tf_op jit(solution)/shard_map/ppermute | solution.py:28
  14.2 305.2 %collective-permute-start.1 = (f32[2,300,2]{2,0,1:T(2,128)}, f32[2,300,2]{2,0,1:T(2,128)}, u32[]{:S(2)}, u32[]{:S(2)}) collective-permute-start(f32[2,300,2]{2,0,1:T(2,128)} %get-tuple-element.71), channel_id=1, source_target_pairs={{4,0},{8,4},{12,8},{16,12},{20,16},{24,20},{28,24},{32,28},{36,32}... | collective-permute-start | bytes 14408 | tf_op jit(solution)/shard_map/ppermute | solution.py:30
  17.2 29.0 %copy-start.53 = (bf16[2,300,256]{2,0,1:T(2,128)(2,1)S(1)}, bf16[2,300,256]{2,0,1:T(2,128)(2,1)}, u32[]{:S(2)}) copy-start(bf16[2,300,256]{2,0,1:T(2,128)(2,1)} %get-tuple-element.68) | copy-start | bytes 921604
  17.2 367.0 %all-gather.19.cloned.1.call-start = ((), (), s32[]{:S(2)}) async-start(), calls=%async_computation.1 | async-start | bytes 1536000 | tf_op jit(solution)/shard_map/all_gather | solution.py:82
  177.9 136.2 %copy-start.93 = (s32[1200]{0:T(1024)S(1)}, s32[1200]{0:T(1024)}, u32[]{:S(2)}) copy-start(s32[1200]{0:T(1024)} %param.13) | copy-start | bytes 14404
  177.9 136.3 %copy-start.91 = (s32[1200]{0:T(1024)S(1)}, s32[1200]{0:T(1024)}, u32[]{:S(2)}) copy-start(s32[1200]{0:T(1024)} %param.14) | copy-start | bytes 14404
  177.9 136.5 %copy-start.92 = (s32[8,8]{1,0:T(8,128)S(1)}, s32[8,8]{1,0:T(8,128)}, u32[]{:S(2)}) copy-start(s32[8,8]{1,0:T(8,128)} %param.15) | copy-start | bytes 772
  187.3 143.1 %copy-start.62 = (f32[1,960]{1,0:T(1,128)}, f32[1,960]{1,0:T(1,128)S(1)}, u32[]{:S(2)}) copy-start(f32[1,960]{1,0:T(1,128)S(1)} %get-tuple-element.87) | copy-start | bytes 11524
  330.4 402.8 %all-gather.21.cloned.1.call-start = ((), (), s32[]{:S(2)}) async-start(), calls=%async_computation.2 | async-start | bytes 1536000 | tf_op jit(solution)/shard_map/all_gather | solution.py:82
  367.9 8.2 collective-permute-start.2
  372.5 8.2 collective-permute-start.3
  390.1 124.3 %copy-start.88 = (f32[2,960]{1,0:T(2,128)S(1)}, f32[2,960]{1,0:T(2,128)}, u32[]{:S(2)}) copy-start(f32[2,960]{1,0:T(2,128)} %fusion.114) | copy-start | bytes 23044
  391.5 376.1 %all-gather.23.cloned.1.call-start = ((), (), s32[]{:S(2)}) async-start(), calls=%async_computation.3 | async-start | bytes 1536000 | tf_op jit(solution)/shard_map/all_gather | solution.py:82
  521.1 52.4 %copy-start.64 = (f32[1,960]{1,0:T(1,128)}, f32[1,960]{1,0:T(1,128)S(1)}, u32[]{:S(2)}) copy-start(f32[1,960]{1,0:T(1,128)S(1)} %get-tuple-element.84) | copy-start | bytes 11524
  521.1 52.4 %copy-start.66 = (f32[1,960]{1,0:T(1,128)}, f32[1,960]{1,0:T(1,128)S(1)}, u32[]{:S(2)}) copy-start(f32[1,960]{1,0:T(1,128)S(1)} %get-tuple-element.85) | copy-start | bytes 11524
  560.4 162.2 %collective-permute-start.4 = (f32[2,300,2]{2,0,1:T(2,128)}, f32[2,300,2]{2,0,1:T(2,128)}, u32[]{:S(2)}, u32[]{:S(2)}) collective-permute-start(f32[2,300,2]{2,0,1:T(2,128)} %get-tuple-element.58), channel_id=1, source_target_pairs={{0,4},{4,8},{8,12},{12,16},{16,20},{20,24},{24,28},{28,32},{32,36}... | collective-permute-start | bytes 14408 | tf_op jit(solution)/shard_map/ppermute | solution.py:28
  573.5 119.9 %copy-start.68 = (f32[1,960]{1,0:T(1,128)}, f32[1,960]{1,0:T(1,128)S(1)}, u32[]{:S(2)}) copy-start(f32[1,960]{1,0:T(1,128)S(1)} %get-tuple-element.82) | copy-start | bytes 11524
  573.5 119.9 %copy-start.70 = (f32[1,960]{1,0:T(1,128)}, f32[1,960]{1,0:T(1,128)S(1)}, u32[]{:S(2)}) copy-start(f32[1,960]{1,0:T(1,128)S(1)} %get-tuple-element.83) | copy-start | bytes 11524
  720.3 9.2 collective-permute-start.5
  740.5 386.7 %all-gather.25.cloned.1.call-start = ((), (), s32[]{:S(2)}) async-start(), calls=%async_computation.4 | async-start | bytes 1536000 | tf_op jit(solution)/shard_map/all_gather | solution.py:82
  753.0 5.7 collective-permute-start.6
  755.0 8.9 collective-permute-start.7
  775.8 386.8 %all-gather.27.cloned.1.call-start = ((), (), s32[]{:S(2)}) async-start(), calls=%async_computation.5 | async-start | bytes 1536000 | tf_op jit(solution)/shard_map/all_gather | solution.py:82
  953.0 163.6 %collective-permute-start.8 = (f32[2,300,2]{2,0,1:T(2,128)}, f32[2,300,2]{2,0,1:T(2,128)}, u32[]{:S(2)}, u32[]{:S(2)}) collective-permute-start(f32[2,300,2]{2,0,1:T(2,128)} %get-tuple-element.46), channel_id=1, source_target_pairs={{0,4},{4,8},{8,12},{12,16},{16,20},{20,24},{24,28},{28,32},{32,36}... | collective-permute-start | bytes 14408 | tf_op jit(solution)/shard_map/ppermute | solution.py:28
  964.7 120.5 %copy-start.76 = (f32[1,960]{1,0:T(1,128)}, f32[1,960]{1,0:T(1,128)S(1)}, u32[]{:S(2)}) copy-start(f32[1,960]{1,0:T(1,128)S(1)} %get-tuple-element.78) | copy-start | bytes 11524
  964.7 120.5 %copy-start.78 = (f32[1,960]{1,0:T(1,128)}, f32[1,960]{1,0:T(1,128)S(1)}, u32[]{:S(2)}) copy-start(f32[1,960]{1,0:T(1,128)S(1)} %get-tuple-element.79) | copy-start | bytes 11524
  1114.2 9.3 collective-permute-start.9
  1135.4 388.1 %all-gather.29.cloned.1.call-start = ((), (), s32[]{:S(2)}) async-start(), calls=%async_computation.6 | async-start | bytes 1536000 | tf_op jit(solution)/shard_map/all_gather | solution.py:82
  1148.0 5.7 collective-permute-start.10
  1150.0 8.9 collective-permute-start.11
  1170.8 523.8 %all-gather.31.cloned.1.call-start = ((), (), s32[]{:S(2)}) async-start(), calls=%async_computation.7 | async-start | bytes 1536000 | tf_op jit(solution)/shard_map/all_gather | solution.py:82
  1349.0 163.9 %collective-permute-start.12 = (f32[2,300,2]{2,0,1:T(2,128)}, f32[2,300,2]{2,0,1:T(2,128)}, u32[]{:S(2)}, u32[]{:S(2)}) collective-permute-start(f32[2,300,2]{2,0,1:T(2,128)} %get-tuple-element.34), channel_id=1, source_target_pairs={{0,4},{4,8},{8,12},{12,16},{16,20},{20,24},{24,28},{28,32},{32,36}... | collective-permute-start | bytes 14408 | tf_op jit(solution)/shard_map/ppermute | solution.py:28
  1360.8 120.7 %copy-start.84 = (f32[1,960]{1,0:T(1,128)}, f32[1,960]{1,0:T(1,128)S(1)}, u32[]{:S(2)}) copy-start(f32[1,960]{1,0:T(1,128)S(1)} %get-tuple-element.74) | copy-start | bytes 11524
  1360.8 120.7 %copy-start.86 = (f32[1,960]{1,0:T(1,128)}, f32[1,960]{1,0:T(1,128)S(1)}, u32[]{:S(2)}) copy-start(f32[1,960]{1,0:T(1,128)S(1)} %get-tuple-element.75) | copy-start | bytes 11524
  1510.5 9.3 collective-permute-start.13
  1666.4 21.3 %copy-start.67 = (f32[1,960]{1,0:T(1,128)S(1)}, f32[1,960]{1,0:T(1,128)}, u32[]{:S(2)}) copy-start(f32[1,960]{1,0:T(1,128)} %copy-done.66) | copy-start | bytes 11524
  1666.4 21.3 %copy-start.69 = (f32[1,960]{1,0:T(1,128)S(1)}, f32[1,960]{1,0:T(1,128)}, u32[]{:S(2)}) copy-start(f32[1,960]{1,0:T(1,128)} %copy-done.68) | copy-start | bytes 11524
  1666.4 21.3 %copy-start.71 = (f32[1,960]{1,0:T(1,128)S(1)}, f32[1,960]{1,0:T(1,128)}, u32[]{:S(2)}) copy-start(f32[1,960]{1,0:T(1,128)} %copy-done.70) | copy-start | bytes 11524
  1666.4 21.3 %copy-start.73 = (f32[1,960]{1,0:T(1,128)S(1)}, f32[1,960]{1,0:T(1,128)}, u32[]{:S(2)}) copy-start(f32[1,960]{1,0:T(1,128)} %copy-done.72) | copy-start | bytes 11524
  1666.4 21.3 %copy-start.75 = (f32[1,960]{1,0:T(1,128)S(1)}, f32[1,960]{1,0:T(1,128)}, u32[]{:S(2)}) copy-start(f32[1,960]{1,0:T(1,128)} %copy-done.74) | copy-start | bytes 11524
  1666.4 21.3 %copy-start.77 = (f32[1,960]{1,0:T(1,128)S(1)}, f32[1,960]{1,0:T(1,128)}, u32[]{:S(2)}) copy-start(f32[1,960]{1,0:T(1,128)} %copy-done.76) | copy-start | bytes 11524
  1666.4 21.3 %copy-start.79 = (f32[1,960]{1,0:T(1,128)S(1)}, f32[1,960]{1,0:T(1,128)}, u32[]{:S(2)}) copy-start(f32[1,960]{1,0:T(1,128)} %copy-done.78) | copy-start | bytes 11524
  1666.4 21.3 %copy-start.81 = (f32[1,960]{1,0:T(1,128)S(1)}, f32[1,960]{1,0:T(1,128)}, u32[]{:S(2)}) copy-start(f32[1,960]{1,0:T(1,128)} %copy-done.80) | copy-start | bytes 11524
  1666.4 21.3 %copy-start.83 = (f32[1,960]{1,0:T(1,128)S(1)}, f32[1,960]{1,0:T(1,128)}, u32[]{:S(2)}) copy-start(f32[1,960]{1,0:T(1,128)} %copy-done.82) | copy-start | bytes 11524
  1666.4 21.3 %copy-start.85 = (f32[1,960]{1,0:T(1,128)S(1)}, f32[1,960]{1,0:T(1,128)}, u32[]{:S(2)}) copy-start(f32[1,960]{1,0:T(1,128)} %copy-done.84) | copy-start | bytes 11524
  1669.3 19.0 %collective-permute-start.14 = (f32[2,300,2]{2,0,1:T(2,128)}, f32[2,300,2]{2,0,1:T(2,128)}, u32[]{:S(2)}, u32[]{:S(2)}) collective-permute-start(f32[2,300,2]{2,0,1:T(2,128)} %get-tuple-element.28), channel_id=1, source_target_pairs={{0,4},{4,8},{8,12},{12,16},{16,20},{20,24},{24,28},{28,32},{32,36}... | collective-permute-start | bytes 14408 | tf_op jit(solution)/shard_map/ppermute | solution.py:28
  1672.9 17.0 collective-permute-start.15
  (70 other events, 331.3 us)
Sparse Core Ops, SparseCore 0:
  17.3 25.8 all-gather.16
  330.5 22.5 all-gather.18
  391.6 23.4 all-gather.20
  740.6 22.7 all-gather.22
  775.9 24.1 all-gather.24
  1135.5 23.9 all-gather.26
  1170.9 25.3 all-gather.28
  1531.8 23.9 all-gather.30
where the time goes:
time: 1720 us; the launch traced here: 1710 us
  blocking collectives  1370 us (80%)
  matrix products  110 us (6%)
  other arithmetic  99.7 us (6%)
  starting transfers between devices  52.4 us (3%)
  waiting for transfers between devices  33.5 us (2%)
  local copies, waits for them, and re-layouts  28.6 us (2%)
    psum x5, blocking collectives, from_root(): return lax.psum(jnp.where(mine, array, jnp.zeros_like(array)), axis)  612 us
    psum x4, blocking collectives, local(): ghost = lax.psum(ghost_part, 'radial')  483 us
    all_gather x8, blocking collectives, local(): lax.all_gather(inner_term.astype(jnp.bfloat16), 'radial', axis=1, tiled=T...  218 us
    dot_general x8, matrix products, local(): jnp.einsum('ij,sj->si', inner_ham, column_block, preferred_element_type=j...  76.7 us
    psum x8, blocking collectives, local(): inner_apply = lax.psum(inner_part, 'chan')  59.2 us
  transfers between devices with their start and end apart: 24, of which 9 were waited for; matrix products, arithmetic and copies ran while one was open for 10% of the time, Pallas kernels for 0%

commit v1 on v0

v1 whole, which is shorter than its diff:
```python
import jax
import jax.numpy as jnp
from jax import lax
from jax.experimental import pallas as pl
from jax.experimental.pallas import tpu as pltpu
from jax.sharding import PartitionSpec as P

ORDER = 8
time_step = 0.008
grid_step = 0.08
inner_radius = 20.0
surface_gain = 16.0 / (24.0 * grid_step * grid_step)
lap_gain = 1.0 / (24.0 * grid_step * grid_step)

MESH = pl.DeviceIdType.MESH
F32, BF16 = jnp.float32, jnp.bfloat16
NRAD, NCH = 32, 4
ROWS, LC, PTS = 960, 300, 256
RP, CP = 1024, 384
SLOTS = 4
HALO, BLK = 16, 64
CR = 320
STRIP = 32
NT = (((1,), (1,)), ((), ()))


def nt_dot(a, b):
    return lax.dot_general(a, b, NT, preferred_element_type=F32)


def nn_dot(a, b):
    return jnp.dot(a, b, preferred_element_type=F32)


def bytes_wait(ref, sem):
    pltpu.make_async_copy(ref, ref, sem).wait()


def row_iota(shape):
    return lax.broadcasted_iota(jnp.int32, shape, 0)


def pack(a):
    row = row_iota((8, 128))
    halves = []
    for h in range(2):
        t = a[:, 512 * h : 512 * h + 128]
        for q in range(1, 4):
            piece = a[:, 512 * h + 128 * q : 512 * h + 128 * (q + 1)]
            t = jnp.where(row // 2 == q, pltpu.roll(piece, 2 * q, 0), t)
        halves.append(t)
    return halves


def unpack(lo, hi):
    out = []
    for h in (lo, hi):
        for q in range(4):
            out.append(h if q == 0 else pltpu.roll(h, 8 - 2 * q, 0))
    return out


def times_minus_i(t, f):
    even = row_iota((8, 128)) % 2 == 0
    return jnp.where(even, f * pltpu.roll(t, 7, 0), -f * pltpu.roll(t, 1, 0))


def kernel(
    ham_hbm, surf, cloc, outer, v0, lmom,
    out_ref, inner_ref,
    hamv, opad, ut, u, uh, call, total, fin,
    vsend, vrec, ysend, yrec, itot, gsend, grec, esend, erec, strip, stot, strec,
    ham_sem, vs_sem, vr_sem, ys_sem, yr_sem, gs_sem, gr_sem, es_sem, er_sem, ss_sem, sr_sem,
    hs_sem, hr_sem, us_sem, ur_sem, cs_sem, cr_sem, fs_sem, fr_sem, loc_sem,
):
    r, c = lax.axis_index("radial"), lax.axis_index("chan")
    z, x, core = r // 8, lax.rem(r, 8) // 2, lax.rem(r, 2)
    is_root = r == 0
    self_plane = c == z
    up, down = lax.rem(r + 1, NRAD), lax.rem(r + NRAD - 1, NRAD)

    zero_rows = jnp.zeros((4, 64, 1920), BF16)
    hamv[:, 0:64, :] = zero_rows
    hamv[:, ROWS:RP, :] = zero_rows

    def ham_copy(i):
        return pltpu.make_async_copy(
            ham_hbm.at[:, pl.ds(1920 * i, 1920)],
            hamv.at[i, pl.ds(pl.multiple_of(64 * core, 64), ROWS)],
            ham_sem.at[i],
        )

    for i in range(4):
        ham_copy(i).start()

    barrier = pltpu.get_barrier_semaphore()

    def greet(device):
        pl.semaphore_signal(barrier, inc=1, device_id=device, device_id_type=MESH)

    for i in range(8):
        for y in range(NCH):
            producer = 8 * c + i

            @pl.when(jnp.logical_or(producer != r, c != y))
            def _():
                greet((producer, y))

    for d in range(1, NCH):
        greet((r, lax.rem(c + d, NCH)))
    greet((up, c))
    greet((down, c))

    @pl.when(is_root)
    def _():
        for d in range(1, NRAD):
            greet((d, c))

    @pl.when(jnp.logical_not(is_root))
    def _():
        greet((0, c))

    opad[:, 256:CP, :] = jnp.zeros((2, CP - 256, PTS), F32)
    opad[:, 0:LC, :] = outer[...]
    for s in range(2):
        for cb in range(3):
            for pb in range(2):
                ut[s, HALO + 128 * pb : HALO + 128 * (pb + 1), 128 * cb : 128 * (cb + 1)] = opad[
                    s, 128 * cb : 128 * (cb + 1), 128 * pb : 128 * (pb + 1)
                ].T
    u[:, :, 0:8, :] = jnp.zeros((NCH, 2, 8, CP), F32)
    u[:, :, 104:112, :] = jnp.zeros((NCH, 2, 8, CP), F32)
    for i in range(NCH):
        call[i, CR:CP, :] = jnp.zeros((CP - CR, NCH * CP), BF16)
    total[...] = jnp.zeros_like(total)
    itot[...] = jnp.zeros_like(itot)

    greeted = 37 - self_plane.astype(jnp.int32) + jnp.where(is_root, NRAD - 1, 1)
    pl.semaphore_wait(barrier, greeted)

    def send_term(k, lo, hi, inner):
        ps, slot = lax.rem(k, 2), lax.rem(k, SLOTS)

        @pl.when(k >= 2)
        def _():
            bytes_wait(yrec.at[0, pl.ds(0, 3)], ys_sem.at[ps])

            @pl.when(self_plane)
            def _():
                bytes_wait(vrec.at[0, pl.ds(0, 31)], vs_sem.at[ps])

            @pl.when(jnp.logical_not(self_plane))
            def _():
                bytes_wait(vrec.at[0], vs_sem.at[ps])

        both = jnp.concatenate([lo, hi], axis=0)
        ysend[ps] = both
        yrec[slot, c] = both

        def send_rows():
            vsend[ps] = both.astype(BF16)
            place = vrec.at[slot, 8 * x + 4 * core + c]

            def remote(rr):
                pltpu.make_async_remote_copy(
                    src_ref=vsend.at[ps],
                    dst_ref=place,
                    send_sem=vs_sem.at[ps],
                    recv_sem=vr_sem.at[slot, x],
                    device_id=(rr, z),
                    device_id_type=MESH,
                ).start()

            for dz in (2, 1, 3, 0):
                for dx in (2, 1, 3, 0):
                    for dc in (1, 0):
                        rr = 8 * lax.rem(z + dz, 4) + 2 * lax.rem(x + dx, 4) + lax.rem(core + dc, 2)
                        if dz or dx or dc:
                            remote(rr)
                        else:

                            @pl.when(self_plane)
                            def _():
                                pltpu.make_async_copy(vsend.at[ps], place, vr_sem.at[slot, x]).start()

                            @pl.when(jnp.logical_not(self_plane))
                            def _():
                                remote(rr)

        def send_peers():
            for d in (2, 1, 3):
                pltpu.make_async_remote_copy(
                    src_ref=ysend.at[ps],
                    dst_ref=yrec.at[slot, c],
                    send_sem=ys_sem.at[ps],
                    recv_sem=yr_sem.at[slot],
                    device_id=(r, lax.rem(c + d, NCH)),
                    device_id_type=MESH,
                ).start()

        send_peers()
        if inner is True:
            send_rows()
        else:
            pl.when(inner)(send_rows)

    def send_edge(k, rows):
        slot = lax.rem(k, SLOTS)
        for i in range(4):
            erec[slot, i : i + 1, :] = rows[i]
        for d in range(1, NRAD):
            pltpu.make_async_remote_copy(
                src_ref=erec.at[slot],
                dst_ref=erec.at[slot],
                send_sem=es_sem.at[slot],
                recv_sem=er_sem.at[slot],
                device_id=((d * 11) % NRAD, c),
                device_id_type=MESH,
            ).start()

    def send_strip(k):
        slot = lax.rem(k, SLOTS)
        for s in range(2):
            strec[slot, c, STRIP * s : STRIP * (s + 1), :] = strip[s, 8 : 8 + STRIP, :].astype(BF16)
        for d in (2, 1, 3):
            pltpu.make_async_remote_copy(
                src_ref=strec.at[slot, c],
                dst_ref=strec.at[slot, c],
                send_sem=ss_sem.at[slot],
                recv_sem=sr_sem.at[slot],
                device_id=(0, lax.rem(c + d, NCH)),
                device_id_type=MESH,
            ).start()

    lo, hi = pack(v0[...] * 0.25)
    send_term(0, lo, hi, True)

    @pl.when(is_root)
    def _():
        strip[...] = jnp.zeros_like(strip)
        for s in range(2):
            strip[s, 8 : 8 + STRIP, :] = ut[s, HALO : HALO + STRIP, :]
        stot[...] = jnp.zeros_like(stot)
        send_edge(0, [strip[s, 8 + m : 9 + m, :] for m in range(2) for s in range(2)])
        send_strip(0)

    def halo_copies():
        low = pltpu.make_async_remote_copy(
            src_ref=ut.at[:, pl.ds(HALO, HALO)], dst_ref=ut.at[:, pl.ds(HALO + PTS, HALO)],
            send_sem=hs_sem.at[0], recv_sem=hr_sem.at[0], device_id=(down, c), device_id_type=MESH,
        )
        high = pltpu.make_async_remote_copy(
            src_ref=ut.at[:, pl.ds(PTS, HALO)], dst_ref=ut.at[:, pl.ds(0, HALO)],
            send_sem=hs_sem.at[1], recv_sem=hr_sem.at[1], device_id=(up, c), device_id_type=MESH,
        )
        return low, high

    for cp in halo_copies():
        cp.start()

    def block_copy(d):
        cc = lax.rem(c + d, NCH)
        return pltpu.make_async_remote_copy(
            src_ref=ut.at[:, pl.ds(pl.multiple_of(BLK * cc, BLK), BLK + 2 * HALO)],
            dst_ref=u.at[c, :, pl.ds(8, BLK + 2 * HALO)],
            send_sem=us_sem.at[d - 1], recv_sem=ur_sem.at[d - 1],
            device_id=(r, cc), device_id_type=MESH,
        )

    def coupling_copy(d):
        return pltpu.make_async_remote_copy(
            src_ref=cloc.at[pl.ds(0, CR)],
            dst_ref=call.at[c, pl.ds(0, CR)],
            send_sem=cs_sem.at[d - 1], recv_sem=cr_sem.at[d - 1],
            device_id=(r, lax.rem(c + d, NCH)), device_id_type=MESH,
        )

    def final_copy(d):
        cc = lax.rem(c + d, NCH)
        return pltpu.make_async_remote_copy(
            src_ref=total.at[cc], dst_ref=fin.at[c],
            send_sem=fs_sem.at[d - 1], recv_sem=fr_sem.at[d - 1],
            device_id=(r, cc), device_id_type=MESH,
        )

    def own_block():
        return ut[:, pl.ds(pl.multiple_of(BLK * c, BLK), BLK + 2 * HALO), :]

    def outer_step(k):
        f = time_step / lax.convert_element_type(k, F32)
        for cp in range(NCH):
            for s in range(2):
                uh[cp, 96 * s : 96 * (s + 1), :] = u[cp, s, 8:104, :].astype(BF16)
        point = PTS * r + BLK * c - HALO + row_iota((96, 1))
        valid = jnp.logical_and(point >= 0, point < NRAD * PTS)
        radius = inner_radius + grid_step * (point.astype(F32) + 1.0)
        inv = 1.0 / (radius * radius)

        def chunk(cc, _):
            mixed = jnp.zeros((192, CP), F32)
            for cp in range(NCH):
                mixed += nn_dot(uh[cp], call[cp, :, pl.ds(pl.multiple_of(CP * cc, CP), CP)])
            applied = []
            for s in range(2):
                w = u[cc, s, 8:104, :]
                lap = (
                    (u[cc, s, 6:102, :] + u[cc, s, 10:106, :])
                    - 16.0 * (u[cc, s, 7:103, :] + u[cc, s, 9:105, :])
                    + 30.0 * w
                )
                applied.append(
                    lap_gain * lap + (lmom[pl.ds(cc, 1), :] * inv) * w + radius * mixed[96 * s : 96 * (s + 1)]
                )
            new = (jnp.where(valid, f * applied[1], 0.0), jnp.where(valid, -f * applied[0], 0.0))
            for s in range(2):
                u[cc, s, 8:104, :] = new[s]
                total[cc, s] += new[s][HALO : HALO + BLK]
            return 0

        lax.fori_loop(0, NCH, chunk, 0)

    def take_peers(k):
        slot = lax.rem(k, SLOTS)
        bytes_wait(yrec.at[slot, pl.ds(0, 3)], yr_sem.at[slot])
        own = (yrec[slot, 0] + yrec[slot, 1]) + (yrec[slot, 2] + yrec[slot, 3])
        itot[...] += own
        return own

    def step(k, _):
        ps, slot, before = lax.rem(k, 2), lax.rem(k, SLOTS), lax.rem(k + SLOTS - 1, SLOTS)
        f = time_step / lax.convert_element_type(k, F32)

        own = take_peers(k - 1)
        rows = jnp.concatenate(unpack(own[0:8], own[8:16]), axis=1).astype(BF16)
        g0, g1 = nt_dot(rows, surf[0]), nt_dot(rows, surf[1])
        ghost = jnp.where(row_iota((8, CP)) < 2, g0, pltpu.roll(g1, 2, 0))[0:4]

        @pl.when(is_root)
        def _():
            grec[slot, 0] = ghost

        @pl.when(jnp.logical_not(is_root))
        def _():
            @pl.when(k >= 3)
            def _():
                bytes_wait(grec.at[0, 0], gs_sem.at[ps])

            gsend[ps] = ghost
            pltpu.make_async_remote_copy(
                src_ref=gsend.at[ps], dst_ref=grec.at[slot, r],
                send_sem=gs_sem.at[ps], recv_sem=gr_sem.at[slot],
                device_id=(0, c), device_id_type=MESH,
            ).start()

        acc = jnp.zeros((8, RP), F32)
        for off in (0, 1, 3, 2):
            xi = lax.rem(x + off, 4)
            bytes_wait(vrec.at[before, pl.ds(8 * xi, 8)], vr_sem.at[before, xi])

            @pl.when(k == 1)
            def _():
                pltpu.make_async_copy(ham_hbm.at[:, pl.ds(0, 1920)], hamv.at[0, pl.ds(0, ROWS)], ham_sem.at[xi]).wait()

            tiles = []
            for co in range(2):
                parts = [vrec[before, 8 * xi + 4 * co + y].astype(F32) for y in range(NCH)]
                both = (parts[0] + parts[1]) + (parts[2] + parts[3])
                tiles.append(unpack(both[0:8], both[8:16]))
            lanes = tiles[0][:7] + [tiles[0][7] + tiles[1][0]] + tiles[1][1:]
            lhs = jnp.concatenate(lanes, axis=1).astype(BF16)
            acc += nt_dot(lhs, hamv[xi])

        @pl.when(jnp.logical_not(is_root))
        def _():
            bytes_wait(erec.at[before], er_sem.at[before])

        edge = jnp.concatenate([erec[before], jnp.zeros((4, CP), F32)], axis=0).astype(BF16)
        acc += surface_gain * (nn_dot(edge, surf[0]) + pltpu.roll(nn_dot(edge, surf[1]), 6, 0))
        lo, hi = pack(acc)
        send_term(k, times_minus_i(lo, f), times_minus_i(hi, f), k < ORDER)

        @pl.when(is_root)
        def _():
            bytes_wait(strec.at[before, pl.ds(0, 3)], sr_sem.at[before])
            mixed = jnp.zeros((2 * STRIP, CP), F32)
            for cp in range(NCH):
                mixed += nt_dot(strec[before, cp], cloc[:, CP * cp : CP * (cp + 1)])
            bytes_wait(grec.at[slot, pl.ds(0, NRAD - 1)], gr_sem.at[slot])
            seen = jnp.zeros((4, CP), F32)
            for i in range(NRAD):
                seen += grec[slot, i]
            for s in range(2):
                strip[s, 7:8, :] = seen[s : s + 1]
                strip[s, 6:7, :] = seen[2 + s : 3 + s]
            radius = inner_radius + grid_step * (row_iota((STRIP, 1)).astype(F32) + 1.0)
            inv = 1.0 / (radius * radius)
            applied = []
            for s in range(2):
                w = strip[s, 8 : 8 + STRIP, :]
                lap = (
                    (strip[s, 6 : 6 + STRIP, :] + strip[s, 10 : 10 + STRIP, :])
                    - 16.0 * (strip[s, 7 : 7 + STRIP, :] + strip[s, 9 : 9 + STRIP, :])
                    + 30.0 * w
                )
                applied.append(
                    lap_gain * lap + (lmom[pl.ds(c, 1), :] * inv) * w + radius * mixed[STRIP * s : STRIP * (s + 1)]
                )
            new = (f * applied[1], -f * applied[0])
            for s in range(2):
                strip[s, 8 : 8 + STRIP, :] = new[s]
                stot[s] += new[s]
            bytes_wait(strec.at[0, pl.ds(0, 3)], ss_sem.at[before])
            bytes_wait(grec.at[0, pl.ds(0, NRAD - 1)], es_sem.at[before])

            @pl.when(k < ORDER)
            def _():
                send_edge(k, [new[s][m : m + 1] for m in range(2) for s in range(2)])
                send_strip(k)

        @pl.when(k == 1)
        def _():
            for cp in halo_copies():
                cp.wait()

            @pl.when(r == NRAD - 1)
            def _():
                ut[:, HALO + PTS :, :] = jnp.zeros((2, HALO, CP), F32)

            for d in (2, 1, 3):
                block_copy(d).start()
            for d in (2, 1, 3):
                coupling_copy(d).start()
            u[c, :, 8:104, :] = own_block()
            call[c, 0:CR, :] = cloc[0:CR, :]

        return 0

    lax.fori_loop(1, ORDER + 1, step, 0)

    for d in (1, 2, 3):
        block_copy(d).wait()
    for d in (1, 2, 3):
        coupling_copy(d).wait()

    def outer_loop(k, _):
        outer_step(k)
        return 0

    lax.fori_loop(1, ORDER + 1, outer_loop, 0)
    for d in (2, 1, 3):
        final_copy(d).start()
    fin[c] = total[c]
    take_peers(ORDER)
    inner_ref[...] = jnp.concatenate(unpack(itot[0:8], itot[8:16]), axis=1)
    for d in (1, 2, 3):
        final_copy(d).wait()

    @pl.when(is_root)
    def _():
        for s in range(2):
            fin[0, s, 0:HALO, :] = stot[s, 0:HALO, :]

    for s in range(2):
        for pb in range(2):
            rows = jnp.concatenate([fin[2 * pb, s], fin[2 * pb + 1, s]], axis=0)
            for cb in range(3):
                n = min(128, LC - 128 * cb)
                out_ref[s, 128 * cb : 128 * cb + n, 128 * pb : 128 * (pb + 1)] = (
                    outer[s, 128 * cb : 128 * cb + n, 128 * pb : 128 * (pb + 1)]
                    + rows[:, 128 * cb : 128 * (cb + 1)].T[0:n]
                )

    @pl.when(self_plane)
    def _():
        bytes_wait(vrec.at[0, pl.ds(0, 31)], vs_sem.at[(ORDER - 1) % 2])

    @pl.when(jnp.logical_not(self_plane))
    def _():
        bytes_wait(vrec.at[0], vs_sem.at[(ORDER - 1) % 2])

    for k in (ORDER - 1, ORDER):
        bytes_wait(yrec.at[0, pl.ds(0, 3)], ys_sem.at[k % 2])

        @pl.when(jnp.logical_not(is_root))
        def _():
            bytes_wait(grec.at[0, 0], gs_sem.at[k % 2])


def local(outer_wave, inner_wave, inner_ham, surface, dipole, ang_mom, target, couple_mask):
    chan = lax.axis_index("chan")
    core = lax.rem(lax.axis_index("radial"), 2)
    pad_c = ((0, 0), (0, CP - LC))
    mom = jnp.pad(ang_mom.reshape(NCH, LC), pad_c, constant_values=-9)
    tgt = jnp.pad(target.reshape(NCH, LC), pad_c, constant_values=-1)
    levels = jnp.arange(couple_mask.shape[0])
    hot = (tgt.reshape(-1)[:, None] == levels[None, :]).astype(BF16)
    hot_mine = lax.dynamic_slice_in_dim(hot, chan * CP, CP, 0)
    allowed = nn_dot(nn_dot(hot_mine, couple_mask.astype(BF16)).astype(BF16), hot.T)
    mom_mine = lax.dynamic_slice_in_dim(mom.reshape(-1), chan * CP, CP, 0)
    step_l = jnp.abs(mom_mine[:, None] - mom.reshape(-1)[None, :]) == 1
    dip = jnp.pad(dipole.reshape(LC, NCH, LC), ((0, CP - LC), (0, 0), (0, CP - LC))).reshape(CP, NCH * CP)
    cloc = jnp.where(step_l & (allowed > 0.5), dip, jnp.zeros_like(dip))
    lvals = mom.astype(F32)
    lmom = jnp.where(mom >= 0, lvals * (lvals + 1.0) / 2.0, 0.0)
    shift = RP - ROWS

    def shifted(a, *front):
        return jnp.where(
            core == 1, jnp.pad(a, front + ((shift, 0),)), jnp.pad(a, front + ((0, shift),))
        )

    surf = shifted(surface, (0, 0), (0, CP - LC))
    v0 = shifted(inner_wave, (0, 6))

    vm = pl.BlockSpec(memory_space=pltpu.VMEM)
    dma = pltpu.SemaphoreType.DMA
    out, inner = pl.pallas_call(
        kernel,
        out_shape=(
            jax.ShapeDtypeStruct((2, LC, PTS), F32),
            jax.ShapeDtypeStruct((8, RP), F32),
        ),
        in_specs=[pl.BlockSpec(memory_space=pl.ANY)] + [vm] * 5,
        out_specs=(vm, vm),
        scratch_shapes=[
            pltpu.VMEM((4, RP, 1920), BF16),
            pltpu.VMEM((2, CP, PTS), F32),
            pltpu.VMEM((2, PTS + 2 * HALO, CP), F32),
            pltpu.VMEM((NCH, 2, 112, CP), F32),
            pltpu.VMEM((NCH, 192, CP), BF16),
            pltpu.VMEM((NCH, CP, NCH * CP), BF16),
            pltpu.VMEM((NCH, 2, BLK, CP), F32),
            pltpu.VMEM((NCH, 2, BLK, CP), F32),
            pltpu.VMEM((2, 16, 128), BF16),
            pltpu.VMEM((SLOTS, 32, 16, 128), BF16),
            pltpu.VMEM((2, 16, 128), F32),
            pltpu.VMEM((SLOTS, NCH, 16, 128), F32),
            pltpu.VMEM((16, 128), F32),
            pltpu.VMEM((2, 4, CP), F32),
            pltpu.VMEM((SLOTS, NRAD, 4, CP), F32),
            pltpu.VMEM((2, 4, CP), F32),
            pltpu.VMEM((SLOTS, 4, CP), F32),
            pltpu.VMEM((2, 48, CP), F32),
            pltpu.VMEM((2, STRIP, CP), F32),
            pltpu.VMEM((SLOTS, NCH, 2 * STRIP, CP), BF16),
            dma((4,)),
            dma((2,)), dma((SLOTS, 4)),
            dma((2,)), dma((SLOTS,)),
            dma((2,)), dma((SLOTS,)),
            dma((SLOTS,)), dma((SLOTS,)),
            dma((SLOTS,)), dma((SLOTS,)),
            dma((2,)), dma((2,)),
            dma((3,)), dma((3,)),
            dma((3,)), dma((3,)),
            dma((3,)), dma((3,)),
            dma((1,)),
        ],
        compiler_params=pltpu.CompilerParams(
            collective_id=0, has_side_effects=True, vmem_limit_bytes=58 * 2**20
        ),
    )(inner_ham, surf, cloc, outer_wave, v0, lmom)
    inner_next = lax.dynamic_slice(inner, (0, shift * core), (2, ROWS))
    return out, inner_next


def solution(mesh):
    placed = (
        P(None, "chan", "radial"),
        P(None, "radial"),
        P("radial", "chan"),
        P(None, "chan", "radial"),
        P("chan", None),
        P(),
        P(),
        P(),
    )
    return jax.shard_map(
        local,
        mesh=mesh,
        in_specs=placed,
        out_specs=(P(None, "chan", "radial"), P(None, "radial")),
        check_vma=False,
    )
```

time: 1720 us -> 215 us (0.12)
  blocking collectives: 1370 us -> 0 us
  Pallas kernels: 0 us -> 200 us
  matrix products: 110 us -> 2.01 us
  other arithmetic: 99.7 us -> 3.7 us
  starting transfers between devices: 52.4 us -> 0 us
  waiting for transfers between devices: 33.5 us -> 0 us
  local copies, waits for them, and re-layouts: 28.6 us -> 8.57 us
    psum x17 -> x0, blocking collectives: 1150 us -> none  [the longest x5 612 us: from_root(): return lax.psum(jnp.where(mine, array, jnp.zeros_like(array)), axis)]
    all_gather x8 -> x0, blocking collectives: 218 us -> none  [local(): lax.all_gather(inner_term.astype(jnp.bfloat16), 'radial', axis=1, tiled=T...]
    pallas_call x0 -> x1, Pallas kernels: none -> 200 us  [local(): pl.pallas_call(kernel, out_shape=(jax.ShapeDtypeStruct((2, LC, PTS), F32)...]
    dot_general x34 -> x1, matrix products: 110 us -> 2.01 us  [nn_dot(): return jnp.dot(a, b, preferred_element_type=F32)]
    ppermute x16 -> x0, starting transfers between devices: 52.1 us -> none  [the longest x8 29.7 us: with_halo(): lax.ppermute(tail, axis, [(i, (i + 1) % count) for i in range(ends)])]
    ppermute x16 -> x0, waiting for transfers between devices: 33.4 us -> none  [the longest x8 30 us: with_halo(): lax.ppermute(head, axis, [((i + 1) % count, i) for i in range(ends)])]
    add x11 -> x0, other arithmetic: 30.4 us -> none  [the longest x8 25.2 us: local(): outer_apply = -0.5 * lap + centri * outer_term + radius * mixed]
    concatenate x7 -> x0, other arithmetic: 26.4 us -> none  [local(): padded = jnp.concatenate([lower, padded[:, :, 2:]], axis=-1)]
  transfers between devices with their start and end apart: 24 -> 0, of which waited for: 9 -> 0; matrix products, arithmetic and copies ran while one was open for 10% -> 0% of each run, Pallas kernels for 0% -> 0%
where the time goes in v1:
time: 215 us
  Pallas kernels  200 us (93%)
  local copies, waits for them, and re-layouts  8.57 us (4%)
  other arithmetic  3.7 us (2%)
    pallas_call x1, Pallas kernels, local(): pl.pallas_call(kernel, out_shape=(jax.ShapeDtypeStruct((2, LC, PTS), F32)...  200 us
    unnamed x16, local copies, waits for them, and re-layouts  5.55 us

profile of v1, /device:TPU:1, one launch (start us, length us, event | category | flops | bytes accessed | tf_op | source)
XLA Modules:
  0.0 215.2 jit_solution(9036020456588303948)
XLA Ops:
  0.6 1.6 copy.10
  2.2 0.0 copy-start
  2.3 2.1 pad_select_fusion.surf
  4.4 0.0 copy-done
  4.4 0.9 reshape.25
  5.3 0.5 pad.31
  5.7 0.0 copy-start.2
  5.7 0.0 copy-start.3
  5.8 0.0 copy-start.5
  5.8 0.2 copy.14
  6.0 0.5 copy-done.2
  6.4 0.1 reshape.24
  6.5 0.3 iota_compare_fusion
  6.8 0.0 copy-done.3
  6.8 0.1 reshape.22
  6.9 0.1 dynamic_slice.9
  7.0 0.0 copy-done.5
  7.0 0.0 copy-start.1
  7.0 0.0 copy-start.4
  7.0 2.0 fusion.1.cloc
  9.0 0.0 copy-done.1
  9.0 0.9 copy.12.outer
  9.9 0.0 copy-done.4
  9.9 0.7 pad_select_fusion.1.v0
  10.6 0.6 fusion.5.lmom
  11.2 200.2 %shard_map.95 = (f32[2,300,256]{2,1,0:T(8,128)}, f32[8,1024]{1,0:T(8,128)}) custom-call(bf16[960,7680]{1,0:T(8,128)(2,1)} %ham_hbm.1, bf16[2,384,1024]{2,1,0:T(8,128)(2,1)} %pad_select_fusion.surf, bf16[384,1536]{1,0:T(8,128)(2,1)} %fusion.1.cloc, f32[2,300,256]{2,1,0:T(8,128)} %copy.12.outer, f32[8,1024]{1,0:T(8,128)} %pad_select_fusion.1.v0, ...), custom_call_target="tpu_custom_call" | custom-call | tf_op jit(solution)/shard_map/pallas_call | solution.py:517
  211.4 2.4 %copy.13 = f32[2,300,256]{2,0,1:T(2,128)} copy(f32[2,300,256]{2,1,0:T(8,128)} %get-tuple-element.6) | data formatting | bytes 1228800
  213.7 1.4 constant_dynamic-slice_fusion
  (4 shorter events, 0.0 us)
Async XLA Ops:
  2.2 2.2 %copy-start = (bf16[300,1200]{1,0:T(8,128)(2,1)S(1)}, bf16[300,1200]{1,0:T(8,128)(2,1)}, u32[]{:S(2)}) copy-start(bf16[300,1200]{1,0:T(8,128)(2,1)} %param.12) | copy-start | bytes 2160004
  5.7 0.7 copy-start.2
  5.7 1.1 copy-start.3
  5.8 1.3 copy-start.5
  7.0 2.0 copy-start.1
  7.0 2.9 %copy-start.4 = (f32[2,960]{1,0:T(2,128)S(1)}, f32[2,960]{1,0:T(2,128)}, u32[]{:S(2)}) copy-start(f32[2,960]{1,0:T(2,128)} %param.9) | copy-start | bytes 23044

commit v2 on v1

--- a/solution.py
+++ b/solution.py
@@ -68,10 +68,10 @@
 def kernel(
     ham_hbm, surf, cloc, outer, v0, lmom,
     out_ref, inner_ref,
-    hamv, opad, ut, u, uh, call, total, fin,
-    vsend, vrec, ysend, yrec, itot, gsend, grec, esend, erec, strip, stot, strec,
+    stage, hamt, opad, ut, u, uh, call, total, fin,
+    vsend, vrec, ysend, yrec, itot, term, gsend, grec, erec, strip, stot, strec,
     ham_sem, vs_sem, vr_sem, ys_sem, yr_sem, gs_sem, gr_sem, es_sem, er_sem, ss_sem, sr_sem,
-    hs_sem, hr_sem, us_sem, ur_sem, cs_sem, cr_sem, fs_sem, fr_sem, loc_sem,
+    hs_sem, hr_sem, us_sem, ur_sem, cs_sem, cr_sem, ds_sem, dr_sem, fs_sem, fr_sem,
 ):
     r, c = lax.axis_index("radial"), lax.axis_index("chan")
     z, x, core = r // 8, lax.rem(r, 8) // 2, lax.rem(r, 2)
@@ -80,13 +80,13 @@
     up, down = lax.rem(r + 1, NRAD), lax.rem(r + NRAD - 1, NRAD)
 
     zero_rows = jnp.zeros((4, 64, 1920), BF16)
-    hamv[:, 0:64, :] = zero_rows
-    hamv[:, ROWS:RP, :] = zero_rows
+    stage[:, 0:64, :] = zero_rows
+    stage[:, ROWS:RP, :] = zero_rows
 
     def ham_copy(i):
         return pltpu.make_async_copy(
             ham_hbm.at[:, pl.ds(1920 * i, 1920)],
-            hamv.at[i, pl.ds(pl.multiple_of(64 * core, 64), ROWS)],
+            stage.at[i, pl.ds(pl.multiple_of(64 * core, 64), ROWS)],
             ham_sem.at[i],
         )
 
@@ -99,12 +99,11 @@
         pl.semaphore_signal(barrier, inc=1, device_id=device, device_id_type=MESH)
 
     for i in range(8):
-        for y in range(NCH):
-            producer = 8 * c + i
-
-            @pl.when(jnp.logical_or(producer != r, c != y))
-            def _():
-                greet((producer, y))
+        producer = 8 * c + i
+
+        @pl.when(producer != r)
+        def _():
+            greet((producer, c))
 
     for d in range(1, NCH):
         greet((r, lax.rem(c + d, NCH)))
@@ -132,77 +131,55 @@
     u[:, :, 104:112, :] = jnp.zeros((NCH, 2, 8, CP), F32)
     for i in range(NCH):
         call[i, CR:CP, :] = jnp.zeros((CP - CR, NCH * CP), BF16)
+    call[c, 0:CR, :] = cloc[0:CR, :]
     total[...] = jnp.zeros_like(total)
-    itot[...] = jnp.zeros_like(itot)
-
-    greeted = 37 - self_plane.astype(jnp.int32) + jnp.where(is_root, NRAD - 1, 1)
+
+    greeted = 5 + jnp.where(self_plane, NRAD - 1, 0) + jnp.where(is_root, NRAD - 1, 1)
     pl.semaphore_wait(barrier, greeted)
 
-    def send_term(k, lo, hi, inner):
+    def send_term(k, lo, hi):
         ps, slot = lax.rem(k, 2), lax.rem(k, SLOTS)
 
-        @pl.when(k >= 2)
+        @pl.when(k >= 3)
         def _():
             bytes_wait(yrec.at[0, pl.ds(0, 3)], ys_sem.at[ps])
-
-            @pl.when(self_plane)
-            def _():
-                bytes_wait(vrec.at[0, pl.ds(0, 31)], vs_sem.at[ps])
-
-            @pl.when(jnp.logical_not(self_plane))
-            def _():
-                bytes_wait(vrec.at[0], vs_sem.at[ps])
 
         both = jnp.concatenate([lo, hi], axis=0)
         ysend[ps] = both
         yrec[slot, c] = both
-
-        def send_rows():
-            vsend[ps] = both.astype(BF16)
-            place = vrec.at[slot, 8 * x + 4 * core + c]
-
-            def remote(rr):
-                pltpu.make_async_remote_copy(
-                    src_ref=vsend.at[ps],
-                    dst_ref=place,
-                    send_sem=vs_sem.at[ps],
-                    recv_sem=vr_sem.at[slot, x],
-                    device_id=(rr, z),
-                    device_id_type=MESH,
-                ).start()
-
-            for dz in (2, 1, 3, 0):
-                for dx in (2, 1, 3, 0):
-                    for dc in (1, 0):
+        for d in (2, 1, 3):
+            pltpu.make_async_remote_copy(
+                src_ref=ysend.at[ps],
+                dst_ref=yrec.at[slot, c],
+                send_sem=ys_sem.at[ps],
+                recv_sem=yr_sem.at[slot],
+                device_id=(r, lax.rem(c + d, NCH)),
+                device_id_type=MESH,
+            ).start()
+
+    def spread(k):
+        ps, slot = lax.rem(k, 2), lax.rem(k + SLOTS - 1, SLOTS)
+
+        @pl.when(k >= 3)
+        def _():
+            bytes_wait(vrec.at[0, pl.ds(0, 31)], vs_sem.at[ps])
+
+        vsend[ps] = term[...].astype(BF16)
+        place = vrec.at[slot, 2 * x + core]
+        for dz in (2, 1, 3, 0):
+            for dx in (2, 1, 3, 0):
+                for dc in (1, 0):
+                    if dz or dx or dc:
                         rr = 8 * lax.rem(z + dz, 4) + 2 * lax.rem(x + dx, 4) + lax.rem(core + dc, 2)
-                        if dz or dx or dc:
-                            remote(rr)
-                        else:
-
-                            @pl.when(self_plane)
-                            def _():
-                                pltpu.make_async_copy(vsend.at[ps], place, vr_sem.at[slot, x]).start()
-
-                            @pl.when(jnp.logical_not(self_plane))
-                            def _():
-                                remote(rr)
-
-        def send_peers():
-            for d in (2, 1, 3):
-                pltpu.make_async_remote_copy(
-                    src_ref=ysend.at[ps],
-                    dst_ref=yrec.at[slot, c],
-                    send_sem=ys_sem.at[ps],
-                    recv_sem=yr_sem.at[slot],
-                    device_id=(r, lax.rem(c + d, NCH)),
-                    device_id_type=MESH,
-                ).start()
-
-        send_peers()
-        if inner is True:
-            send_rows()
-        else:
-            pl.when(inner)(send_rows)
+                        pltpu.make_async_remote_copy(
+                            src_ref=vsend.at[ps],
+                            dst_ref=place,
+                            send_sem=vs_sem.at[ps],
+                            recv_sem=vr_sem.at[slot, x],
+                            device_id=(rr, c),
+                            device_id_type=MESH,
+                        ).start()
+        pltpu.make_async_copy(vsend.at[ps], place, vr_sem.at[slot, x]).start()
 
     def send_edge(k, rows):
         slot = lax.rem(k, SLOTS)
@@ -232,8 +209,9 @@
                 device_id_type=MESH,
             ).start()
 
-    lo, hi = pack(v0[...] * 0.25)
-    send_term(0, lo, hi, True)
+    lo, hi = pack(v0[...])
+    term[...] = jnp.concatenate([lo, hi], axis=0)
+    itot[...] = term[...]
 
     @pl.when(is_root)
     def _():
@@ -267,13 +245,48 @@
             device_id=(r, cc), device_id_type=MESH,
         )
 
-    def coupling_copy(d):
-        return pltpu.make_async_remote_copy(
-            src_ref=cloc.at[pl.ds(0, CR)],
-            dst_ref=call.at[c, pl.ds(0, CR)],
-            send_sem=cs_sem.at[d - 1], recv_sem=cr_sem.at[d - 1],
-            device_id=(r, lax.rem(c + d, NCH)), device_id_type=MESH,
-        )
+    half = pl.ds(pl.multiple_of(CR // 2 * core, CR // 2), CR // 2)
+
+    def next_block(p, d):
+        return lax.rem(p + (2 if d == 1 else 1), NCH)
+
+    def columns(i):
+        return pl.ds(pl.multiple_of(CP * i, CP), CP)
+
+    def coupling_copies(d):
+        out = []
+        for j in range(2):
+            cols = columns(c if j == 0 else next_block(c, d))
+            out.append(
+                pltpu.make_async_remote_copy(
+                    src_ref=cloc.at[half, cols],
+                    dst_ref=call.at[c, half, cols],
+                    send_sem=cs_sem.at[2 * d - 2 + j], recv_sem=cr_sem.at[2 * d - 2 + j],
+                    device_id=(r, lax.rem(c + d, NCH)), device_id_type=MESH,
+                )
+            )
+        return out
+
+    def share_copies(d):
+        p = lax.rem(c + NCH - d, NCH)
+        out = []
+        for j in range(2):
+            place = call.at[p, half, columns(p if j == 0 else next_block(p, d))]
+            out.append(
+                pltpu.make_async_remote_copy(
+                    src_ref=place, dst_ref=place,
+                    send_sem=ds_sem.at[2 * d - 2 + j], recv_sem=dr_sem.at[2 * d - 2 + j],
+                    device_id=(r + 1 - 2 * core, c), device_id_type=MESH,
+                )
+            )
+        return out
+
+    def mirror(a, b):
+        call[b, :, columns(a)] = call[a, :, columns(b)].T
+
+    for d in (2, 1, 3):
+        for cp in coupling_copies(d):
+            cp.start()
 
     def final_copy(d):
         cc = lax.rem(c + d, NCH)
@@ -319,19 +332,22 @@
 
         lax.fori_loop(0, NCH, chunk, 0)
 
-    def take_peers(k):
-        slot = lax.rem(k, SLOTS)
-        bytes_wait(yrec.at[slot, pl.ds(0, 3)], yr_sem.at[slot])
-        own = (yrec[slot, 0] + yrec[slot, 1]) + (yrec[slot, 2] + yrec[slot, 3])
-        itot[...] += own
-        return own
+    first = 4
+
+    def outer_when(k, start, index):
+        @pl.when(jnp.logical_and(k >= start, k < start + 4))
+        def _():
+            outer_step(index)
 
     def step(k, _):
         ps, slot, before = lax.rem(k, 2), lax.rem(k, SLOTS), lax.rem(k + SLOTS - 1, SLOTS)
         f = time_step / lax.convert_element_type(k, F32)
 
-        own = take_peers(k - 1)
-        rows = jnp.concatenate(unpack(own[0:8], own[8:16]), axis=1).astype(BF16)
+        @pl.when(self_plane)
+        def _():
+            spread(k)
+
+        rows = jnp.concatenate(unpack(term[0:8], term[8:16]), axis=1).astype(BF16)
         g0, g1 = nt_dot(rows, surf[0]), nt_dot(rows, surf[1])
         ghost = jnp.where(row_iota((8, CP)) < 2, g0, pltpu.roll(g1, 2, 0))[0:4]
 
@@ -352,23 +368,56 @@
                 device_id=(0, c), device_id_type=MESH,
             ).start()
 
+        @pl.when(k == 1)
+        def _():
+            for i in range(4):
+                ham_copy(i).wait()
+
+                def turn(j, _):
+                    at = pl.ds(pl.multiple_of(128 * j, 128), 128)
+                    hamt[i, at, :] = stage[i, :, at].T
+                    return 0
+
+                lax.fori_loop(0, 15, turn, 0)
+
+        @pl.when(k == first - 1)
+        def _():
+            for d in (2, 1, 3):
+                for cp in coupling_copies(d):
+                    cp.wait()
+                for cp in share_copies(d):
+                    cp.start()
+
+        @pl.when(k == first)
+        def _():
+            for d in (2, 1, 3):
+                for cp in share_copies(d):
+                    cp.wait()
+            for d in (1, 2, 3):
+                mirror(c, lax.rem(c + d, NCH))
+                p = lax.rem(c + NCH - d, NCH)
+                mirror(p, next_block(p, d))
+                block_copy(d).wait()
+
+        outer_when(k, first + 1, 2 * (k - first))
+
+        @pl.when(k == first + 4)
+        def _():
+            for d in (2, 1, 3):
+                final_copy(d).start()
+            fin[c] = total[c]
+
         acc = jnp.zeros((8, RP), F32)
         for off in (0, 1, 3, 2):
             xi = lax.rem(x + off, 4)
-            bytes_wait(vrec.at[before, pl.ds(8 * xi, 8)], vr_sem.at[before, xi])
-
-            @pl.when(k == 1)
-            def _():
-                pltpu.make_async_copy(ham_hbm.at[:, pl.ds(0, 1920)], hamv.at[0, pl.ds(0, ROWS)], ham_sem.at[xi]).wait()
-
+            bytes_wait(vrec.at[before, pl.ds(2 * xi, 2)], vr_sem.at[before, xi])
             tiles = []
             for co in range(2):
-                parts = [vrec[before, 8 * xi + 4 * co + y].astype(F32) for y in range(NCH)]
-                both = (parts[0] + parts[1]) + (parts[2] + parts[3])
+                both = vrec[before, 2 * xi + co].astype(F32)
                 tiles.append(unpack(both[0:8], both[8:16]))
             lanes = tiles[0][:7] + [tiles[0][7] + tiles[1][0]] + tiles[1][1:]
             lhs = jnp.concatenate(lanes, axis=1).astype(BF16)
-            acc += nt_dot(lhs, hamv[xi])
+            acc += nn_dot(lhs, hamt[xi])
 
         @pl.when(jnp.logical_not(is_root))
         def _():
@@ -377,7 +426,7 @@
         edge = jnp.concatenate([erec[before], jnp.zeros((4, CP), F32)], axis=0).astype(BF16)
         acc += surface_gain * (nn_dot(edge, surf[0]) + pltpu.roll(nn_dot(edge, surf[1]), 6, 0))
         lo, hi = pack(acc)
-        send_term(k, times_minus_i(lo, f), times_minus_i(hi, f), k < ORDER)
+        send_term(k, times_minus_i(lo, f), times_minus_i(hi, f))
 
         @pl.when(is_root)
         def _():
@@ -428,29 +477,18 @@
 
             for d in (2, 1, 3):
                 block_copy(d).start()
-            for d in (2, 1, 3):
-                coupling_copy(d).start()
             u[c, :, 8:104, :] = own_block()
-            call[c, 0:CR, :] = cloc[0:CR, :]
-
+
+        outer_when(k, first, 2 * (k - first) + 1)
+
+        bytes_wait(yrec.at[slot, pl.ds(0, 3)], yr_sem.at[slot])
+        own = (yrec[slot, 0] + yrec[slot, 1]) + (yrec[slot, 2] + yrec[slot, 3])
+        itot[...] += own
+        term[...] = own
         return 0
 
     lax.fori_loop(1, ORDER + 1, step, 0)
 
-    for d in (1, 2, 3):
-        block_copy(d).wait()
-    for d in (1, 2, 3):
-        coupling_copy(d).wait()
-
-    def outer_loop(k, _):
-        outer_step(k)
-        return 0
-
-    lax.fori_loop(1, ORDER + 1, outer_loop, 0)
-    for d in (2, 1, 3):
-        final_copy(d).start()
-    fin[c] = total[c]
-    take_peers(ORDER)
     inner_ref[...] = jnp.concatenate(unpack(itot[0:8], itot[8:16]), axis=1)
     for d in (1, 2, 3):
         final_copy(d).wait()
@@ -470,16 +508,12 @@
                     + rows[:, 128 * cb : 128 * (cb + 1)].T[0:n]
                 )
 
-    @pl.when(self_plane)
-    def _():
-        bytes_wait(vrec.at[0, pl.ds(0, 31)], vs_sem.at[(ORDER - 1) % 2])
-
-    @pl.when(jnp.logical_not(self_plane))
-    def _():
-        bytes_wait(vrec.at[0], vs_sem.at[(ORDER - 1) % 2])
-
     for k in (ORDER - 1, ORDER):
         bytes_wait(yrec.at[0, pl.ds(0, 3)], ys_sem.at[k % 2])
+
+        @pl.when(self_plane)
+        def _():
+            bytes_wait(vrec.at[0, pl.ds(0, 31)], vs_sem.at[k % 2])
 
         @pl.when(jnp.logical_not(is_root))
         def _():
@@ -524,6 +558,7 @@
         out_specs=(vm, vm),
         scratch_shapes=[
             pltpu.VMEM((4, RP, 1920), BF16),
+            pltpu.VMEM((4, 1920, RP), BF16),
             pltpu.VMEM((2, CP, PTS), F32),
             pltpu.VMEM((2, PTS + 2 * HALO, CP), F32),
             pltpu.VMEM((NCH, 2, 112, CP), F32),
@@ -536,9 +571,9 @@
             pltpu.VMEM((2, 16, 128), F32),
             pltpu.VMEM((SLOTS, NCH, 16, 128), F32),
             pltpu.VMEM((16, 128), F32),
+            pltpu.VMEM((16, 128), F32),
             pltpu.VMEM((2, 4, CP), F32),
             pltpu.VMEM((SLOTS, NRAD, 4, CP), F32),
-            pltpu.VMEM((2, 4, CP), F32),
             pltpu.VMEM((SLOTS, 4, CP), F32),
             pltpu.VMEM((2, 48, CP), F32),
             pltpu.VMEM((2, STRIP, CP), F32),
@@ -551,9 +586,9 @@
             dma((SLOTS,)), dma((SLOTS,)),
             dma((2,)), dma((2,)),
             dma((3,)), dma((3,)),
+            dma((6,)), dma((6,)),
+            dma((6,)), dma((6,)),
             dma((3,)), dma((3,)),
-            dma((3,)), dma((3,)),
-            dma((1,)),
         ],
         compiler_params=pltpu.CompilerParams(
             collective_id=0, has_side_effects=True, vmem_limit_bytes=58 * 2**20

time: 215 us -> 121 us (0.56)
  Pallas kernels: 200 us -> 106 us
    pallas_call x1, Pallas kernels: 200 us -> 106 us  [local(): pl.pallas_call(kernel, out_shape=(jax.ShapeDtypeStruct((2, LC, PTS), F32)...]
where the time goes in v2:
time: 121 us
  Pallas kernels  106 us (88%)
  local copies, waits for them, and re-layouts  8.57 us (7%)
  other arithmetic  3.7 us (3%)
  matrix products  2.01 us (2%)
    pallas_call x1, Pallas kernels, local(): pl.pallas_call(kernel, out_shape=(jax.ShapeDtypeStruct((2, LC, PTS), F32)...  106 us
    unnamed x16, local copies, waits for them, and re-layouts  5.55 us
    select_n x2, other arithmetic, shifted(): jnp.where(core == 1, jnp.pad(a, front + ((shift, 0),)), jnp.pad(a, front...  2.83 us

profile of v2, /device:TPU:1, one launch (start us, length us, event | category | flops | bytes accessed | tf_op | source)
XLA Modules:
  0.0 121.1 jit_solution(1877267593449386225)
XLA Ops:
  0.6 1.6 %copy.10 = bf16[2,300,960]{2,1,0:T(8,128)(2,1)S(1)} copy(bf16[2,300,960]{2,0,1:T(2,128)(2,1)} %param.11) | data formatting | bytes 2304000 | tf_op args[3]
  2.2 0.0 copy-start
  2.3 2.1 %pad_select_fusion.surf = bf16[2,384,1024]{2,1,0:T(8,128)(2,1)} fusion(bf16[2,300,960]{2,1,0:T(8,128)(2,1)S(1)} %copy.10, pred[]{:T(512)S(6)} %eq.25), kind=kLoop, calls=%fused_computation.4 | loop fusion | flops 786432 | bytes 2724865 | tf_op jit(solution)/shard_map/jit(_where)/select_n | solution.py:542
  4.4 0.0 copy-done
  4.4 0.9 reshape.25
  5.3 0.5 pad.31
  5.7 0.0 copy-start.2
  5.7 0.0 copy-start.3
  5.8 0.0 copy-start.5
  5.8 0.2 copy.14
  6.0 0.5 copy-done.2
  6.4 0.1 reshape.24
  6.5 0.3 iota_compare_fusion
  6.8 0.0 copy-done.3
  6.8 0.1 reshape.22
  6.9 0.1 dynamic_slice.9
  7.0 0.0 copy-done.5
  7.0 0.0 copy-start.1
  7.0 0.0 copy-start.4
  7.0 2.0 %fusion.1.cloc = bf16[384,1536]{1,0:T(8,128)(2,1)} fusion(bf16[384,1536]{1,0:T(8,128)(2,1)S(1)} %bitcast.4, pred[1536,8]{1,0:T(32,128)(4,1)S(1)} %iota_compare_fusion, s32[1536]{0:T(1024)S(1)} %reshape.23, s32[384]{0:T(512)S(1)} %dynamic_slice.9, s32[]{:T(128)S(6)} %select_n.33, s32[8,8]{1,0:T(8,128)S(1)} %copy-done.5), kind=kOutput, calls=%fused_computation.3 | convolution fusion | flops 13028416 | bytes 2619396 | tf_op jit(solution)/shard_map/dot_general | solution.py:32
  9.0 0.0 copy-done.1
  9.0 0.9 copy.12.outer
  9.9 0.0 copy-done.4
  9.9 0.7 pad_select_fusion.1.v0
  10.6 0.6 fusion.5.lmom
  11.2 106.1 %shard_map.95 = (f32[2,300,256]{2,1,0:T(8,128)}, f32[8,1024]{1,0:T(8,128)}) custom-call(bf16[960,7680]{1,0:T(8,128)(2,1)} %ham_hbm.1, bf16[2,384,1024]{2,1,0:T(8,128)(2,1)} %pad_select_fusion.surf, bf16[384,1536]{1,0:T(8,128)(2,1)} %fusion.1.cloc, f32[2,300,256]{2,1,0:T(8,128)} %copy.12.outer, f32[8,1024]{1,0:T(8,128)} %pad_select_fusion.1.v0, ...), custom_call_target="tpu_custom_call" | custom-call | tf_op jit(solution)/shard_map/pallas_call | solution.py:551
  117.3 2.4 %copy.13 = f32[2,300,256]{2,0,1:T(2,128)} copy(f32[2,300,256]{2,1,0:T(8,128)} %get-tuple-element.6) | data formatting | bytes 1228800
  119.7 1.4 %constant_dynamic-slice_fusion = f32[2,960]{1,0:T(2,128)} fusion(f32[8,1024]{1,0:T(8,128)} %get-tuple-element.5, s32[]{:T(128)S(6)} %select_n.38), kind=kLoop, calls=%fused_computation.13 | loop fusion | bytes 15364 | tf_op jit(solution)/shard_map/dynamic_slice | solution.py:597
  (4 shorter events, 0.0 us)
Async XLA Ops:
  2.2 2.2 %copy-start = (bf16[300,1200]{1,0:T(8,128)(2,1)S(1)}, bf16[300,1200]{1,0:T(8,128)(2,1)}, u32[]{:S(2)}) copy-start(bf16[300,1200]{1,0:T(8,128)(2,1)} %param.12) | copy-start | bytes 2160004
  5.7 0.7 copy-start.2
  5.7 1.1 copy-start.3
  5.8 1.3 %copy-start.5 = (s32[8,8]{1,0:T(8,128)S(1)}, s32[8,8]{1,0:T(8,128)}, u32[]{:S(2)}) copy-start(s32[8,8]{1,0:T(8,128)} %param.15) | copy-start | bytes 772
  7.0 2.0 %copy-start.1 = (f32[2,300,256]{2,0,1:T(2,128)S(1)}, f32[2,300,256]{2,0,1:T(2,128)}, u32[]{:S(2)}) copy-start(f32[2,300,256]{2,0,1:T(2,128)} %param.8) | copy-start | bytes 1843204
  7.0 2.9 %copy-start.4 = (f32[2,960]{1,0:T(2,128)S(1)}, f32[2,960]{1,0:T(2,128)}, u32[]{:S(2)}) copy-start(f32[2,960]{1,0:T(2,128)} %param.9) | copy-start | bytes 23044

commit v3 on v2

--- a/solution.py
+++ b/solution.py
@@ -66,9 +66,9 @@
 
 
 def kernel(
-    ham_hbm, surf, cloc, outer, v0, lmom,
+    ham_hbm, surf_in, dipole, outer, v0, mom, target, couple_mask,
     out_ref, inner_ref,
-    stage, hamt, opad, ut, u, uh, call, total, fin,
+    surf, cloc, dpad, pads, hot, lmom, m64, v0p, stage, hamt, opad, ut, u, uh, mix, call, total, fin,
     vsend, vrec, ysend, yrec, itot, term, gsend, grec, erec, strip, stot, strec,
     ham_sem, vs_sem, vr_sem, ys_sem, yr_sem, gs_sem, gr_sem, es_sem, er_sem, ss_sem, sr_sem,
     hs_sem, hr_sem, us_sem, ur_sem, cs_sem, cr_sem, ds_sem, dr_sem, fs_sem, fr_sem,
@@ -79,6 +79,8 @@
     self_plane = c == z
     up, down = lax.rem(r + 1, NRAD), lax.rem(r + NRAD - 1, NRAD)
 
+    is_first, is_second = core == 0, core == 1
+
     zero_rows = jnp.zeros((4, 64, 1920), BF16)
     stage[:, 0:64, :] = zero_rows
     stage[:, ROWS:RP, :] = zero_rows
@@ -120,19 +122,75 @@
         greet((0, c))
 
     opad[:, 256:CP, :] = jnp.zeros((2, CP - 256, PTS), F32)
-    opad[:, 0:LC, :] = outer[...]
+    for s in range(2):
+        opad[s, 0:LC, :] = outer[:, s, :]
     for s in range(2):
         for cb in range(3):
             for pb in range(2):
                 ut[s, HALO + 128 * pb : HALO + 128 * (pb + 1), 128 * cb : 128 * (cb + 1)] = opad[
                     s, 128 * cb : 128 * (cb + 1), 128 * pb : 128 * (pb + 1)
                 ].T
+    surf[...] = jnp.zeros_like(surf)
+    v0p[...] = jnp.zeros_like(v0p)
+
+    def place_rows(at):
+        for m in range(2):
+            surf[m, 0:LC, at : at + ROWS] = surf_in[:, m, :]
+        v0p[0:2, at : at + ROWS] = v0[...]
+
+    pl.when(is_first)(lambda: place_rows(0))
+    pl.when(is_second)(lambda: place_rows(RP - ROWS))
+
     u[:, :, 0:8, :] = jnp.zeros((NCH, 2, 8, CP), F32)
     u[:, :, 104:112, :] = jnp.zeros((NCH, 2, 8, CP), F32)
     for i in range(NCH):
-        call[i, CR:CP, :] = jnp.zeros((CP - CR, NCH * CP), BF16)
-    call[c, 0:CR, :] = cloc[0:CR, :]
+        call[CP * i + CR : CP * (i + 1), :] = jnp.zeros((CP - CR, NCH * CP), BF16)
     total[...] = jnp.zeros_like(total)
+
+    dpad[...] = jnp.zeros_like(dpad)
+    dpad[0:LC, 0 : NCH * LC] = dipole[...]
+    pads[...] = jnp.full(pads.shape, -1, jnp.int32)
+    pads[0:1, 0 : NCH * LC] = target[...].reshape(1, NCH * LC)
+    pads[1:2, 0 : NCH * LC] = mom[...].reshape(1, NCH * LC)
+    kind = row_iota((64, 1280))
+    features = jnp.where(
+        kind < 32, (kind == pads[0:1, :]).astype(F32), (kind - 32 == pads[1:2, :]).astype(F32)
+    ).astype(BF16)
+    row64, col64 = row_iota((64, 64)), lax.broadcasted_iota(jnp.int32, (64, 64), 1)
+    m64[...] = jnp.where(jnp.logical_and(row64 >= 32, jnp.abs(row64 - col64) == 1), jnp.where(col64 >= 32, 1.0, 0.0), 0.0)
+    m64[0:8, 0:8] = couple_mask[...].astype(F32)
+    moments = jnp.where(row_iota((8, 64)) == 0, lax.broadcasted_iota(jnp.int32, (8, 64), 1) - 32, 0)
+    moments = jnp.where(lax.broadcasted_iota(jnp.int32, (8, 64), 1) >= 32, moments, 0).astype(F32).astype(BF16)
+
+    def selection(i):
+        at = row_iota((512, CP)) + 256 * i - LC * i
+        column = lax.broadcasted_iota(jnp.int32, (512, CP), 1)
+        return jnp.where(jnp.logical_and(at == column, column < LC), 1.0, 0.0).astype(BF16)
+
+    for i in range(NCH):
+        hot[i] = nn_dot(features[:, 256 * i : 256 * i + 512], selection(i))
+        lval = nn_dot(moments, hot[i].astype(BF16))[0:1]
+        lmom[i : i + 1, :] = lval * (lval + 1.0) * 0.5
+    mine = hot[c].T.astype(BF16)
+    for i in range(NCH):
+        met = nn_dot(mine, nn_dot(m64[...].astype(BF16), hot[i].astype(BF16)).astype(BF16))
+        moved = nn_dot(dpad[:, 256 * i : 256 * i + 512], selection(i))
+        cloc[:, CP * i : CP * (i + 1)] = jnp.where(met > 1.5, moved, 0.0).astype(BF16)
+
+    call[pl.ds(pl.multiple_of(CP * c, CP), CP), :] = cloc[...]
+
+    def take_matrix(i):
+        ham_copy(i).wait()
+
+        def turn(j, _):
+            at = pl.ds(pl.multiple_of(128 * j, 128), 128)
+            hamt[i, at, :] = stage[i, :, at].T
+            return 0
+
+        lax.fori_loop(0, 15, turn, 0)
+
+    for i in range(2):
+        take_matrix(i)
 
     greeted = 5 + jnp.where(self_plane, NRAD - 1, 0) + jnp.where(is_root, NRAD - 1, 1)
     pl.semaphore_wait(barrier, greeted)
@@ -209,7 +267,7 @@
                 device_id_type=MESH,
             ).start()
 
-    lo, hi = pack(v0[...])
+    lo, hi = pack(v0p[...])
     term[...] = jnp.concatenate([lo, hi], axis=0)
     itot[...] = term[...]
 
@@ -245,7 +303,8 @@
             device_id=(r, cc), device_id_type=MESH,
         )
 
-    half = pl.ds(pl.multiple_of(CR // 2 * core, CR // 2), CR // 2)
+    def half(i):
+        return pl.ds(pl.multiple_of(CP * i + CR // 2 * core, 32), CR // 2)
 
     def next_block(p, d):
         return lax.rem(p + (2 if d == 1 else 1), NCH)
@@ -259,8 +318,8 @@
             cols = columns(c if j == 0 else next_block(c, d))
             out.append(
                 pltpu.make_async_remote_copy(
-                    src_ref=cloc.at[half, cols],
-                    dst_ref=call.at[c, half, cols],
+                    src_ref=cloc.at[half(0), cols],
+                    dst_ref=call.at[half(c), cols],
                     send_sem=cs_sem.at[2 * d - 2 + j], recv_sem=cr_sem.at[2 * d - 2 + j],
                     device_id=(r, lax.rem(c + d, NCH)), device_id_type=MESH,
                 )
@@ -271,7 +330,7 @@
         p = lax.rem(c + NCH - d, NCH)
         out = []
         for j in range(2):
-            place = call.at[p, half, columns(p if j == 0 else next_block(p, d))]
+            place = call.at[half(p), columns(p if j == 0 else next_block(p, d))]
             out.append(
                 pltpu.make_async_remote_copy(
                     src_ref=place, dst_ref=place,
@@ -282,11 +341,7 @@
         return out
 
     def mirror(a, b):
-        call[b, :, columns(a)] = call[a, :, columns(b)].T
-
-    for d in (2, 1, 3):
-        for cp in coupling_copies(d):
-            cp.start()
+        call[columns(b), columns(a)] = call[columns(a), columns(b)].T
 
     def final_copy(d):
         cc = lax.rem(c + d, NCH)
@@ -303,16 +358,15 @@
         f = time_step / lax.convert_element_type(k, F32)
         for cp in range(NCH):
             for s in range(2):
-                uh[cp, 96 * s : 96 * (s + 1), :] = u[cp, s, 8:104, :].astype(BF16)
+                uh[96 * s : 96 * (s + 1), CP * cp : CP * (cp + 1)] = u[cp, s, 8:104, :].astype(BF16)
+        for h in range(2):
+            mix[:, 768 * h : 768 * (h + 1)] = nn_dot(uh[...], call[:, 768 * h : 768 * (h + 1)])
         point = PTS * r + BLK * c - HALO + row_iota((96, 1))
         valid = jnp.logical_and(point >= 0, point < NRAD * PTS)
         radius = inner_radius + grid_step * (point.astype(F32) + 1.0)
         inv = 1.0 / (radius * radius)
 
         def chunk(cc, _):
-            mixed = jnp.zeros((192, CP), F32)
-            for cp in range(NCH):
-                mixed += nn_dot(uh[cp], call[cp, :, pl.ds(pl.multiple_of(CP * cc, CP), CP)])
             applied = []
             for s in range(2):
                 w = u[cc, s, 8:104, :]
@@ -322,7 +376,7 @@
                     + 30.0 * w
                 )
                 applied.append(
-                    lap_gain * lap + (lmom[pl.ds(cc, 1), :] * inv) * w + radius * mixed[96 * s : 96 * (s + 1)]
+                    lap_gain * lap + (lmom[pl.ds(cc, 1), :] * inv) * w + radius * mix[96 * s : 96 * (s + 1), columns(cc)]
                 )
             new = (jnp.where(valid, f * applied[1], 0.0), jnp.where(valid, -f * applied[0], 0.0))
             for s in range(2):
@@ -370,15 +424,24 @@
 
         @pl.when(k == 1)
         def _():
-            for i in range(4):
-                ham_copy(i).wait()
-
-                def turn(j, _):
-                    at = pl.ds(pl.multiple_of(128 * j, 128), 128)
-                    hamt[i, at, :] = stage[i, :, at].T
-                    return 0
-
-                lax.fori_loop(0, 15, turn, 0)
+            for d in (2, 1, 3):
+                for cp in coupling_copies(d):
+                    cp.start()
+            take_matrix(2)
+
+        @pl.when(k == 1)
+        def _():
+            for cp in halo_copies():
+                cp.wait()
+
+            @pl.when(r == NRAD - 1)
+            def _():
+                ut[:, HALO + PTS :, :] = jnp.zeros((2, HALO, CP), F32)
+
+            for d in (2, 1, 3):
+                block_copy(d).start()
+            u[c, :, 8:104, :] = own_block()
+            take_matrix(3)
 
         @pl.when(k == first - 1)
         def _():
@@ -388,8 +451,7 @@
                 for cp in share_copies(d):
                     cp.start()
 
-        @pl.when(k == first)
-        def _():
+        def take_coupling():
             for d in (2, 1, 3):
                 for cp in share_copies(d):
                     cp.wait()
@@ -399,16 +461,18 @@
                 mirror(p, next_block(p, d))
                 block_copy(d).wait()
 
-        outer_when(k, first + 1, 2 * (k - first))
-
-        @pl.when(k == first + 4)
-        def _():
-            for d in (2, 1, 3):
-                final_copy(d).start()
-            fin[c] = total[c]
+        outer_when(k, first, 2 * (k - first) + 1)
 
         acc = jnp.zeros((8, RP), F32)
         for off in (0, 1, 3, 2):
+            if off == 2:
+                @pl.when(jnp.logical_not(is_root))
+                def _():
+                    bytes_wait(erec.at[before], er_sem.at[before])
+
+                edge = jnp.concatenate([erec[before], jnp.zeros((4, CP), F32)], axis=0).astype(BF16)
+                acc += surface_gain * (nn_dot(edge, surf[0]) + pltpu.roll(nn_dot(edge, surf[1]), 6, 0))
+
             xi = lax.rem(x + off, 4)
             bytes_wait(vrec.at[before, pl.ds(2 * xi, 2)], vr_sem.at[before, xi])
             tiles = []
@@ -419,12 +483,6 @@
             lhs = jnp.concatenate(lanes, axis=1).astype(BF16)
             acc += nn_dot(lhs, hamt[xi])
 
-        @pl.when(jnp.logical_not(is_root))
-        def _():
-            bytes_wait(erec.at[before], er_sem.at[before])
-
-        edge = jnp.concatenate([erec[before], jnp.zeros((4, CP), F32)], axis=0).astype(BF16)
-        acc += surface_gain * (nn_dot(edge, surf[0]) + pltpu.roll(nn_dot(edge, surf[1]), 6, 0))
         lo, hi = pack(acc)
         send_term(k, times_minus_i(lo, f), times_minus_i(hi, f))
 
@@ -466,20 +524,14 @@
                 send_edge(k, [new[s][m : m + 1] for m in range(2) for s in range(2)])
                 send_strip(k)
 
-        @pl.when(k == 1)
-        def _():
-            for cp in halo_copies():
-                cp.wait()
-
-            @pl.when(r == NRAD - 1)
-            def _():
-                ut[:, HALO + PTS :, :] = jnp.zeros((2, HALO, CP), F32)
-
+        pl.when(k == first - 1)(take_coupling)
+        outer_when(k, first, 2 * (k - first) + 2)
+
+        @pl.when(k == first + 3)
+        def _():
             for d in (2, 1, 3):
-                block_copy(d).start()
-            u[c, :, 8:104, :] = own_block()
-
-        outer_when(k, first, 2 * (k - first) + 1)
+                final_copy(d).start()
+            fin[c] = total[c]
 
         bytes_wait(yrec.at[slot, pl.ds(0, 3)], yr_sem.at[slot])
         own = (yrec[slot, 0] + yrec[slot, 1]) + (yrec[slot, 2] + yrec[slot, 3])
@@ -489,7 +541,16 @@
 
     lax.fori_loop(1, ORDER + 1, step, 0)
 
-    inner_ref[...] = jnp.concatenate(unpack(itot[0:8], itot[8:16]), axis=1)
+    inner = jnp.concatenate(unpack(itot[0:8], itot[8:16]), axis=1)[0:2]
+
+    @pl.when(is_first)
+    def _():
+        inner_ref[...] = inner[:, 0:ROWS]
+
+    @pl.when(is_second)
+    def _():
+        inner_ref[...] = inner[:, RP - ROWS : RP]
+
     for d in (1, 2, 3):
         final_copy(d).wait()
 
@@ -503,8 +564,8 @@
             rows = jnp.concatenate([fin[2 * pb, s], fin[2 * pb + 1, s]], axis=0)
             for cb in range(3):
                 n = min(128, LC - 128 * cb)
-                out_ref[s, 128 * cb : 128 * cb + n, 128 * pb : 128 * (pb + 1)] = (
-                    outer[s, 128 * cb : 128 * cb + n, 128 * pb : 128 * (pb + 1)]
+                out_ref[128 * cb : 128 * cb + n, s, 128 * pb : 128 * (pb + 1)] = (
+                    opad[s, 128 * cb : 128 * cb + n, 128 * pb : 128 * (pb + 1)]
                     + rows[:, 128 * cb : 128 * (cb + 1)].T[0:n]
                 )
 
@@ -520,50 +581,39 @@
             bytes_wait(grec.at[0, 0], gs_sem.at[k % 2])
 
 
+def hand_on(out, inner, out_ref, inner_ref):
+    out_ref[...] = out[...]
+    inner_ref[...] = inner[...]
+
+
 def local(outer_wave, inner_wave, inner_ham, surface, dipole, ang_mom, target, couple_mask):
-    chan = lax.axis_index("chan")
-    core = lax.rem(lax.axis_index("radial"), 2)
-    pad_c = ((0, 0), (0, CP - LC))
-    mom = jnp.pad(ang_mom.reshape(NCH, LC), pad_c, constant_values=-9)
-    tgt = jnp.pad(target.reshape(NCH, LC), pad_c, constant_values=-1)
-    levels = jnp.arange(couple_mask.shape[0])
-    hot = (tgt.reshape(-1)[:, None] == levels[None, :]).astype(BF16)
-    hot_mine = lax.dynamic_slice_in_dim(hot, chan * CP, CP, 0)
-    allowed = nn_dot(nn_dot(hot_mine, couple_mask.astype(BF16)).astype(BF16), hot.T)
-    mom_mine = lax.dynamic_slice_in_dim(mom.reshape(-1), chan * CP, CP, 0)
-    step_l = jnp.abs(mom_mine[:, None] - mom.reshape(-1)[None, :]) == 1
-    dip = jnp.pad(dipole.reshape(LC, NCH, LC), ((0, CP - LC), (0, 0), (0, CP - LC))).reshape(CP, NCH * CP)
-    cloc = jnp.where(step_l & (allowed > 0.5), dip, jnp.zeros_like(dip))
-    lvals = mom.astype(F32)
-    lmom = jnp.where(mom >= 0, lvals * (lvals + 1.0) / 2.0, 0.0)
-    shift = RP - ROWS
-
-    def shifted(a, *front):
-        return jnp.where(
-            core == 1, jnp.pad(a, front + ((shift, 0),)), jnp.pad(a, front + ((0, shift),))
-        )
-
-    surf = shifted(surface, (0, 0), (0, CP - LC))
-    v0 = shifted(inner_wave, (0, 6))
-
     vm = pl.BlockSpec(memory_space=pltpu.VMEM)
     dma = pltpu.SemaphoreType.DMA
     out, inner = pl.pallas_call(
         kernel,
         out_shape=(
-            jax.ShapeDtypeStruct((2, LC, PTS), F32),
-            jax.ShapeDtypeStruct((8, RP), F32),
+            jax.ShapeDtypeStruct((LC, 2, PTS), F32),
+            jax.ShapeDtypeStruct((2, ROWS), F32),
         ),
-        in_specs=[pl.BlockSpec(memory_space=pl.ANY)] + [vm] * 5,
+        in_specs=[pl.BlockSpec(memory_space=pl.ANY)] + [vm] * 7,
         out_specs=(vm, vm),
         scratch_shapes=[
+            pltpu.VMEM((2, CP, RP), BF16),
+            pltpu.VMEM((CP, NCH * CP), BF16),
+            pltpu.VMEM((CP, 1280), BF16),
+            pltpu.VMEM((8, 1280), jnp.int32),
+            pltpu.VMEM((NCH, 64, CP), F32),
+            pltpu.VMEM((NCH, CP), F32),
+            pltpu.VMEM((64, 64), F32),
+            pltpu.VMEM((8, RP), F32),
             pltpu.VMEM((4, RP, 1920), BF16),
             pltpu.VMEM((4, 1920, RP), BF16),
             pltpu.VMEM((2, CP, PTS), F32),
             pltpu.VMEM((2, PTS + 2 * HALO, CP), F32),
             pltpu.VMEM((NCH, 2, 112, CP), F32),
-            pltpu.VMEM((NCH, 192, CP), BF16),
-            pltpu.VMEM((NCH, CP, NCH * CP), BF16),
+            pltpu.VMEM((192, NCH * CP), BF16),
+            pltpu.VMEM((192, NCH * CP), F32),
+            pltpu.VMEM((NCH * CP, NCH * CP), BF16),
             pltpu.VMEM((NCH, 2, BLK, CP), F32),
             pltpu.VMEM((NCH, 2, BLK, CP), F32),
             pltpu.VMEM((2, 16, 128), BF16),
@@ -593,9 +643,23 @@
         compiler_params=pltpu.CompilerParams(
             collective_id=0, has_side_effects=True, vmem_limit_bytes=58 * 2**20
         ),
-    )(inner_ham, surf, cloc, outer_wave, v0, lmom)
-    inner_next = lax.dynamic_slice(inner, (0, shift * core), (2, ROWS))
-    return out, inner_next
+    )(
+        inner_ham,
+        jnp.transpose(surface, (1, 0, 2)),
+        dipole,
+        jnp.transpose(outer_wave, (1, 0, 2)),
+        inner_wave,
+        ang_mom,
+        target,
+        couple_mask,
+    )
+    out, inner = pl.pallas_call(
+        hand_on,
+        out_shape=(jax.ShapeDtypeStruct(out.shape, F32), jax.ShapeDtypeStruct(inner.shape, F32)),
+        in_specs=[vm, vm],
+        out_specs=(vm, vm),
+    )(out, inner)
+    return jnp.transpose(out, (1, 0, 2)), inner
 
 
 def solution(mesh):

time: 121 us -> 118 us (0.975)
  Pallas kernels: 106 us -> 117 us
  local copies, waits for them, and re-layouts: 8.57 us -> 0 us
  other arithmetic: 3.7 us -> 0 us
  matrix products: 2.01 us -> 0 us
    pallas_call x1 -> x2, Pallas kernels: 106 us -> 117 us  [the longest x1 115 us: local(): pl.pallas_call(kernel, out_shape=(jax.ShapeDtypeStruct((LC, 2, PTS), F32)...]
    unnamed x16 -> x0, local copies, waits for them, and re-layouts: 5.55 us -> none
    select_n x3 -> x0, other arithmetic: 3.43 us -> none  [the longest x2 2.83 us: shifted(): jnp.where(core == 1, jnp.pad(a, front + ((shift, 0),)), jnp.pad(a, front...]
    dot_general x1 -> x0, matrix products: 2.01 us -> none  [nn_dot(): return jnp.dot(a, b, preferred_element_type=F32)]
    dynamic_slice x2 -> x0, local copies, waits for them, and re-layouts: 1.51 us -> none  [the longest x1 1.43 us: local(): inner_next = lax.dynamic_slice(inner, (0, shift * core), (2, ROWS))]
where the time goes in v3:
time: 118 us
  Pallas kernels  117 us (99%)
    pallas_call x1, Pallas kernels, local(): pl.pallas_call(kernel, out_shape=(jax.ShapeDtypeStruct((LC, 2, PTS), F32)...  115 us

profile of v3, /device:TPU:1, one launch (start us, length us, event | category | flops | bytes accessed | tf_op | source)
XLA Modules:
  0.0 117.9 jit_solution(1394995046892457055)
XLA Ops:
  0.6 115.3 %shard_map.95 = (f32[300,2,256]{2,1,0:T(2,128)}, f32[2,960]{1,0:T(2,128)}) custom-call(bf16[960,7680]{1,0:T(8,128)(2,1)} %ham_hbm.1, bf16[300,2,960]{2,1,0:T(2,128)(2,1)} %bitcast.3, bf16[300,1200]{1,0:T(8,128)(2,1)} %dipole.1, f32[300,2,256]{2,1,0:T(2,128)} %bitcast.4, f32[2,960]{1,0:T(2,128)} %v0.1, s32[1200]{0:T(1024)} %mom.1, s32[1200]{0:T(1024)} %target.1, ...), custom_call_target="tpu_custom_call" | custom-call | tf_op jit(solution)/shard_map/pallas_call | solution.py:592
  115.9 1.9 %shard_map.96 = (f32[300,2,256]{2,1,0:T(2,128)}, f32[2,960]{1,0:T(2,128)}) custom-call(f32[300,2,256]{2,1,0:T(2,128)} %get-tuple-element.6.out, f32[2,960]{1,0:T(2,128)} %get-tuple-element.7.inner), custom_call_target="tpu_custom_call" | custom-call | tf_op jit(solution)/shard_map/pallas_call | solution.py:656

commit v4 on v3

--- a/solution.py
+++ b/solution.py
@@ -294,12 +294,12 @@
     for cp in halo_copies():
         cp.start()
 
-    def block_copy(d):
+    def block_copy(d, s):
         cc = lax.rem(c + d, NCH)
         return pltpu.make_async_remote_copy(
-            src_ref=ut.at[:, pl.ds(pl.multiple_of(BLK * cc, BLK), BLK + 2 * HALO)],
-            dst_ref=u.at[c, :, pl.ds(8, BLK + 2 * HALO)],
-            send_sem=us_sem.at[d - 1], recv_sem=ur_sem.at[d - 1],
+            src_ref=ut.at[s, pl.ds(pl.multiple_of(BLK * cc, BLK), BLK + 2 * HALO)],
+            dst_ref=u.at[c, s, pl.ds(8, BLK + 2 * HALO)],
+            send_sem=us_sem.at[2 * d - 2 + s], recv_sem=ur_sem.at[2 * d - 2 + s],
             device_id=(r, cc), device_id_type=MESH,
         )
 
@@ -438,18 +438,29 @@
             def _():
                 ut[:, HALO + PTS :, :] = jnp.zeros((2, HALO, CP), F32)
 
-            for d in (2, 1, 3):
-                block_copy(d).start()
             u[c, :, 8:104, :] = own_block()
             take_matrix(3)
 
-        @pl.when(k == first - 1)
-        def _():
+        @pl.when(k == 2)
+        def _():
+            for d in (2, 1, 3):
+                block_copy(d, 0).start()
             for d in (2, 1, 3):
                 for cp in coupling_copies(d):
                     cp.wait()
                 for cp in share_copies(d):
                     cp.start()
+
+        @pl.when(k == 3)
+        def _():
+            for d in (2, 1, 3):
+                block_copy(d, 1).start()
+
+        @pl.when(k == first + 4)
+        def _():
+            for d in (2, 1, 3):
+                final_copy(d).start()
+            fin[c] = total[c]
 
         def take_coupling():
             for d in (2, 1, 3):
@@ -459,7 +470,8 @@
                 mirror(c, lax.rem(c + d, NCH))
                 p = lax.rem(c + NCH - d, NCH)
                 mirror(p, next_block(p, d))
-                block_copy(d).wait()
+                block_copy(d, 0).wait()
+                block_copy(d, 1).wait()
 
         outer_when(k, first, 2 * (k - first) + 1)
 
@@ -526,12 +538,6 @@
 
         pl.when(k == first - 1)(take_coupling)
         outer_when(k, first, 2 * (k - first) + 2)
-
-        @pl.when(k == first + 3)
-        def _():
-            for d in (2, 1, 3):
-                final_copy(d).start()
-            fin[c] = total[c]
 
         bytes_wait(yrec.at[slot, pl.ds(0, 3)], yr_sem.at[slot])
         own = (yrec[slot, 0] + yrec[slot, 1]) + (yrec[slot, 2] + yrec[slot, 3])
@@ -635,7 +641,7 @@
             dma((SLOTS,)), dma((SLOTS,)),
             dma((SLOTS,)), dma((SLOTS,)),
             dma((2,)), dma((2,)),
-            dma((3,)), dma((3,)),
+            dma((6,)), dma((6,)),
             dma((6,)), dma((6,)),
             dma((6,)), dma((6,)),
             dma((3,)), dma((3,)),

time: 118 us -> 107 us (0.907)
  Pallas kernels: 117 us -> 106 us
    pallas_call x1, Pallas kernels: 115 us -> 104 us  [local(): pl.pallas_call(kernel, out_shape=(jax.ShapeDtypeStruct((LC, 2, PTS), F32)...]
where the time goes in v4:
time: 107 us; the launch traced here: 106 us
  Pallas kernels  106 us (99%)
    pallas_call x1, Pallas kernels, local(): pl.pallas_call(kernel, out_shape=(jax.ShapeDtypeStruct((LC, 2, PTS), F32)...  104 us

profile of v4, /device:TPU:1, one launch (start us, length us, event | category | flops | bytes accessed | tf_op | source)
XLA Modules:
  0.0 106.5 jit_solution(3044183721141656212)
XLA Ops:
  0.6 103.9 %shard_map.95 = (f32[300,2,256]{2,1,0:T(2,128)}, f32[2,960]{1,0:T(2,128)}) custom-call(bf16[960,7680]{1,0:T(8,128)(2,1)} %ham_hbm.1, bf16[300,2,960]{2,1,0:T(2,128)(2,1)} %bitcast.3, bf16[300,1200]{1,0:T(8,128)(2,1)} %dipole.1, f32[300,2,256]{2,1,0:T(2,128)} %bitcast.4, f32[2,960]{1,0:T(2,128)} %v0.1, s32[1200]{0:T(1024)} %mom.1, s32[1200]{0:T(1024)} %target.1, ...), custom_call_target="tpu_custom_call" | custom-call | tf_op jit(solution)/shard_map/pallas_call | solution.py:598
  104.6 1.9 %shard_map.96 = (f32[300,2,256]{2,1,0:T(2,128)}, f32[2,960]{1,0:T(2,128)}) custom-call(f32[300,2,256]{2,1,0:T(2,128)} %get-tuple-element.6.out, f32[2,960]{1,0:T(2,128)} %get-tuple-element.7.inner), custom_call_target="tpu_custom_call" | custom-call | tf_op jit(solution)/shard_map/pallas_call | solution.py:662

commit v5 on v4

--- a/solution.py
+++ b/solution.py
@@ -189,8 +189,6 @@
 
         lax.fori_loop(0, 15, turn, 0)
 
-    for i in range(2):
-        take_matrix(i)
 
     greeted = 5 + jnp.where(self_plane, NRAD - 1, 0) + jnp.where(is_root, NRAD - 1, 1)
     pl.semaphore_wait(barrier, greeted)
@@ -427,6 +425,8 @@
             for d in (2, 1, 3):
                 for cp in coupling_copies(d):
                     cp.start()
+            take_matrix(0)
+            take_matrix(1)
             take_matrix(2)
 
         @pl.when(k == 1)

time: 107 us -> 103 us (0.963)
  Pallas kernels: 106 us -> 102 us
    pallas_call x1, Pallas kernels: 104 us -> 100 us  [local(): pl.pallas_call(kernel, out_shape=(jax.ShapeDtypeStruct((LC, 2, PTS), F32)...]
where the time goes in v5:
time: 103 us
  Pallas kernels  102 us (99%)
    pallas_call x1, Pallas kernels, local(): pl.pallas_call(kernel, out_shape=(jax.ShapeDtypeStruct((LC, 2, PTS), F32)...  100 us

profile of v5, /device:TPU:1, one launch (start us, length us, event | category | flops | bytes accessed | tf_op | source)
XLA Modules:
  0.0 103.0 jit_solution(2540576331243390559)
XLA Ops:
  0.6 100.4 %shard_map.95 = (f32[300,2,256]{2,1,0:T(2,128)}, f32[2,960]{1,0:T(2,128)}) custom-call(bf16[960,7680]{1,0:T(8,128)(2,1)} %ham_hbm.1, bf16[300,2,960]{2,1,0:T(2,128)(2,1)} %bitcast.3, bf16[300,1200]{1,0:T(8,128)(2,1)} %dipole.1, f32[300,2,256]{2,1,0:T(2,128)} %bitcast.4, f32[2,960]{1,0:T(2,128)} %v0.1, s32[1200]{0:T(1024)} %mom.1, s32[1200]{0:T(1024)} %target.1, ...), custom_call_target="tpu_custom_call" | custom-call | tf_op jit(solution)/shard_map/pallas_call | solution.py:598
  101.0 1.9 %shard_map.96 = (f32[300,2,256]{2,1,0:T(2,128)}, f32[2,960]{1,0:T(2,128)}) custom-call(f32[300,2,256]{2,1,0:T(2,128)} %get-tuple-element.6.out, f32[2,960]{1,0:T(2,128)} %get-tuple-element.7.inner), custom_call_target="tpu_custom_call" | custom-call | tf_op jit(solution)/shard_map/pallas_call | solution.py:662

commit v6 on v5

--- a/solution.py
+++ b/solution.py
@@ -341,11 +341,11 @@
     def mirror(a, b):
         call[columns(b), columns(a)] = call[columns(a), columns(b)].T
 
-    def final_copy(d):
+    def final_copy(d, s):
         cc = lax.rem(c + d, NCH)
         return pltpu.make_async_remote_copy(
-            src_ref=total.at[cc], dst_ref=fin.at[c],
-            send_sem=fs_sem.at[d - 1], recv_sem=fr_sem.at[d - 1],
+            src_ref=total.at[cc, s], dst_ref=fin.at[c, s],
+            send_sem=fs_sem.at[2 * d - 2 + s], recv_sem=fr_sem.at[2 * d - 2 + s],
             device_id=(r, cc), device_id_type=MESH,
         )
 
@@ -459,7 +459,7 @@
         @pl.when(k == first + 4)
         def _():
             for d in (2, 1, 3):
-                final_copy(d).start()
+                final_copy(d, 1).start()
             fin[c] = total[c]
 
         def take_coupling():
@@ -539,6 +539,11 @@
         pl.when(k == first - 1)(take_coupling)
         outer_when(k, first, 2 * (k - first) + 2)
 
+        @pl.when(k == first + 3)
+        def _():
+            for d in (2, 1, 3):
+                final_copy(d, 0).start()
+
         bytes_wait(yrec.at[slot, pl.ds(0, 3)], yr_sem.at[slot])
         own = (yrec[slot, 0] + yrec[slot, 1]) + (yrec[slot, 2] + yrec[slot, 3])
         itot[...] += own
@@ -558,7 +563,8 @@
         inner_ref[...] = inner[:, RP - ROWS : RP]
 
     for d in (1, 2, 3):
-        final_copy(d).wait()
+        final_copy(d, 0).wait()
+        final_copy(d, 1).wait()
 
     @pl.when(is_root)
     def _():
@@ -644,7 +650,7 @@
             dma((6,)), dma((6,)),
             dma((6,)), dma((6,)),
             dma((6,)), dma((6,)),
-            dma((3,)), dma((3,)),
+            dma((6,)), dma((6,)),
         ],
         compiler_params=pltpu.CompilerParams(
             collective_id=0, has_side_effects=True, vmem_limit_bytes=58 * 2**20

time: 103 us -> 103 us (level)
  no operation moved by 1% of the time
where the time goes in v6:
time: 103 us; the launch traced here: 102 us
  Pallas kernels  102 us (99%)
    pallas_call x1, Pallas kernels, local(): pl.pallas_call(kernel, out_shape=(jax.ShapeDtypeStruct((LC, 2, PTS), F32)...  99.8 us

profile of v6, /device:TPU:1, one launch (start us, length us, event | category | flops | bytes accessed | tf_op | source)
XLA Modules:
  0.0 102.3 jit_solution(10067482714428397214)
XLA Ops:
  0.6 99.8 %shard_map.95 = (f32[300,2,256]{2,1,0:T(2,128)}, f32[2,960]{1,0:T(2,128)}) custom-call(bf16[960,7680]{1,0:T(8,128)(2,1)} %ham_hbm.1, bf16[300,2,960]{2,1,0:T(2,128)(2,1)} %bitcast.3, bf16[300,1200]{1,0:T(8,128)(2,1)} %dipole.1, f32[300,2,256]{2,1,0:T(2,128)} %bitcast.4, f32[2,960]{1,0:T(2,128)} %v0.1, s32[1200]{0:T(1024)} %mom.1, s32[1200]{0:T(1024)} %target.1, ...), custom_call_target="tpu_custom_call" | custom-call | tf_op jit(solution)/shard_map/pallas_call | solution.py:604
  100.4 1.9 %shard_map.96 = (f32[300,2,256]{2,1,0:T(2,128)}, f32[2,960]{1,0:T(2,128)}) custom-call(f32[300,2,256]{2,1,0:T(2,128)} %get-tuple-element.6.out, f32[2,960]{1,0:T(2,128)} %get-tuple-element.7.inner), custom_call_target="tpu_custom_call" | custom-call | tf_op jit(solution)/shard_map/pallas_call | solution.py:668
